TPU v7x, 128 devices: a whole 4x4x4 slice. The times are simulated.
128 devices in a mesh: section: 16 (over y, z_hi, core), peer: 8 (over x, z_lo).
Axes of the slice: x: 4, y: 4, z: 4 (z_hi: 2, z_lo: 2; z = z_hi * 2 + z_lo), core: 2. Of those that a mesh axis runs over, the one named last changes fastest.
Arguments:
- codes: bfloat16 [32768, 1024], P(('section', 'peer')), may hold values from -6 to 6
- routes: int32 [128, 2], P(('section', 'peer')), may hold values from 0 to 7, as said below
- w_up: bfloat16 [16, 1024, 4096], P('section'), may hold values from -0.1875 to 0.1875
- w_down: bfloat16 [16, 4096, 1024], P('section'), may hold values from -0.09375 to 0.09375
- cotangent: bfloat16 [65536, 1024], P(('section', 'peer')), may hold values from -6 to 6
Outputs:
- next_codes: bfloat16 [65536, 1024], P(('section', 'peer'))
- code_grads: bfloat16 [32768, 1024], P(('section', 'peer'))
- up_grad: bfloat16 [16, 1024, 4096], P('section', 'peer')
- down_grad: bfloat16 [16, 4096, 1024], P('section', 'peer')
Inputs may be any that keep to these rules, and one draw needn't show every extreme that they name: `routes`: each sender's 2 blocks go to different peers. In every section every peer receives at least one block and at most 4, and some peer receives exactly 4.
All inputs are finite; a program needn't handle non-finite values.
Results may differ from a plain program's by a relative error of at most 0.019.
Values may be sent and summed in bfloat16 or wider, within the bound.
A program may use at most 256 MiB of HBM per device.

v0:
```python
import jax
import jax.numpy as jnp
from jax import lax
from jax.sharding import PartitionSpec as P

eps = 1e-05


def passed_along(array, axis, by):
    devices = lax.axis_size(axis)
    return lax.ppermute(array, axis, [(i, (i + by) % devices) for i in range(devices)])


def layer(inputs, up_w, down_w, cot):
    x = jnp.dot(inputs, up_w, preferred_element_type=jnp.float32)
    r = lax.rsqrt(jnp.mean(x * x, axis=-1, keepdims=True) + eps)
    z = x * r
    act = jax.nn.silu(z).astype(jnp.bfloat16)
    y = jnp.dot(act, down_w, preferred_element_type=jnp.float32)
    out = (inputs.astype(jnp.float32) + y).astype(jnp.bfloat16)
    back = lax.dot_general(
        cot, down_w, (((1,), (1,)), ((), ())), preferred_element_type=jnp.float32
    )
    sig = jax.nn.sigmoid(z)
    dz = back * sig * (1.0 + z * (1.0 - sig))
    dx = (r * dz - x * (r * r * r) * jnp.mean(x * dz, axis=-1, keepdims=True)).astype(jnp.bfloat16)
    in_grad = lax.dot_general(
        dx, up_w, (((1,), (1,)), ((), ())), preferred_element_type=jnp.float32
    )
    in_grad = (in_grad + cot.astype(jnp.float32)).astype(jnp.bfloat16)
    return (out, act, dx, in_grad)


def route_onehot(row, peers):
    return (row[None, :] == jnp.arange(peers, dtype=jnp.int32)[:, None]).astype(jnp.bfloat16)


def slot_matrix(table, target, slots):
    live = jnp.any(table == target, axis=1)
    rank = jnp.cumsum(live.astype(jnp.int32)) - 1
    sel = live[None, :] & (rank[None, :] == jnp.arange(slots, dtype=jnp.int32)[:, None])
    return sel.astype(jnp.bfloat16)


def apply_matrix(matrix, flat):
    return jnp.dot(matrix, flat, preferred_element_type=jnp.float32).astype(jnp.bfloat16)


def shards(codes, routes, w_up, w_down, cotangent):
    peers = lax.axis_size("peer")
    own_peer = lax.axis_index("peer")
    nblk = routes.shape[1]
    width = codes.shape[1]
    blk = codes.shape[0] // nblk
    slots = cotangent.shape[0] // blk
    blocks = codes.reshape(nblk, blk * width)
    up_w = w_up[0]
    down_w = w_down[0]
    table = lax.all_gather(routes, "peer", axis=0, tiled=True)
    sending = route_onehot(routes[0], peers)
    buffer = apply_matrix(sending, blocks).reshape(peers, blk, width)
    arrived = lax.all_to_all(buffer, "peer", split_axis=0, concat_axis=0, tiled=True)
    select = slot_matrix(table, own_peer, slots)
    packed = apply_matrix(select, arrived.reshape(peers, blk * width))
    inputs = passed_along(packed, "section", 1).reshape(slots * blk, width)
    out, act, dx, in_grad = layer(inputs, up_w, down_w, cotangent)
    homeward = passed_along(in_grad.reshape(slots, blk * width), "section", -1)
    spread = apply_matrix(select.T, homeward).reshape(peers, blk, width)
    returned = lax.all_to_all(spread, "peer", split_axis=0, concat_axis=0, tiled=True)
    sent_grads = apply_matrix(sending.T, returned.reshape(peers, blk * width))
    factor = 1.0 / (peers * nblk)
    contract = (((0,), (0,)), ((), ()))
    part_rows = inputs
    up_total = lax.psum_scatter(
        lax.dot_general(part_rows, dx, contract, preferred_element_type=jnp.float32).astype(
            jnp.bfloat16
        ),
        "peer",
        scatter_dimension=0,
        tiled=True,
    ).astype(jnp.float32)
    part_rows = act
    down_total = lax.psum_scatter(
        lax.dot_general(part_rows, cotangent, contract, preferred_element_type=jnp.float32).astype(
            jnp.bfloat16
        ),
        "peer",
        scatter_dimension=0,
        tiled=True,
    ).astype(jnp.float32)
    up_grad = (up_total * factor).astype(jnp.bfloat16)[None]
    down_grad = (down_total * factor).astype(jnp.bfloat16)[None]
    return (out, sent_grads.reshape(nblk * blk, width), up_grad, down_grad)


def solution(mesh):
    placed = (
        P(("section", "peer"), None),
        P(("section", "peer"), None),
        P("section", None, None),
        P("section", None, None),
        P(("section", "peer"), None),
    )
    return jax.shard_map(
        shards,
        mesh=mesh,
        in_specs=placed,
        out_specs=(
            P(("section", "peer"), None),
            P(("section", "peer"), None),
            P("section", "peer", None),
            P("section", "peer", None),
        ),
        check_vma=False,
    )
```

profile of v0, /device:TPU:1, one launch (start us, length us, event | category | flops | bytes accessed | tf_op | source)
XLA Modules:
  0.0 492.3 jit_solution(1988944176557780995)
XLA Ops:
  7.2 0.0 copy-start.2
  7.2 1.4 reshape.83
  8.6 1.3 convolution_convert_fusion.1
  10.0 2.5 copy.9
  12.5 6.2 %all-to-all-start = ((bf16[8,128,1024]{2,1,0:T(8,128)(2,1)}), bf16[8,128,1024]{2,1,0:T(8,128)(2,1)S(1)}, u32[]{:S(2)}, u32[]{:S(2)}) async-start(bf16[8,128,1024]{2,1,0:T(8,128)(2,1)} %copy.9), calls=%async_computation | async-start | bytes 4194304 | tf_op jit(solution)/shard_map/all_to_all | solution.py:62
  18.7 0.0 reduce-scatter.3.cloned.1.call-start
  18.7 0.0 copy-done.2
  18.7 35.2 %all-gather = s32[8,1,2]{2,1,0:T(1,128)S(1)} all-gather(s32[1,1,2]{2,1,0:T(1,128)S(1)} %bitcast.53), channel_id=1, replica_groups=mesh['section'=16,'peer'=8] {'peer'}, dimensions={0}, use_global_device_ids=true | all-gather | bytes 72 | tf_op jit(solution)/shard_map/all_gather | solution.py:59
  53.9 0.2 compare_reduce_fusion
  54.2 0.2 reduce-window.8
  54.4 0.0 all-to-all-done
  54.4 1.2 copy.11
  55.5 0.7 convolution_convert_fusion.2
  56.2 7.6 %collective-permute-start = (bf16[4,131072]{1,0:T(4,128)(2,1)S(1)}, bf16[4,131072]{1,0:T(4,128)(2,1)S(1)}, u32[]{:S(2)}, u32[]{:S(2)}) collective-permute-start(bf16[4,131072]{1,0:T(4,128)(2,1)S(1)} %convolution_convert_fusion.2), channel_id=1, source_target_pairs={{0,8},{8,16},{16,24},{24,32},{32,40},{40,48},{48,56},{56,64},{64,7... | collective-permute-start | bytes 3145736 | tf_op jit(solution)/shard_map/ppermute | solution.py:11
  63.8 11.7 %collective-permute-done = bf16[4,131072]{1,0:T(4,128)(2,1)S(1)} collective-permute-done((bf16[4,131072]{1,0:T(4,128)(2,1)S(1)}, bf16[4,131072]{1,0:T(4,128)(2,1)S(1)}, u32[]{:S(2)}, u32[]{:S(2)}) %collective-permute-start) | collective-permute-done | bytes 1048608 | tf_op jit(solution)/shard_map/ppermute | solution.py:11
  75.6 0.9 reshape.86
  76.5 0.0 copy-start.3
  76.5 7.1 %multiply_reduce_fusion.1 = (f32[512]{0:T(512)S(1)}, f32[512,4096]{1,0:T(8,128)S(1)}) fusion(bf16[512,1024]{1,0:T(8,128)(2,1)S(1)} %reshape.86, bf16[1,1024,4096]{2,1,0:T(8,128)(2,1)} %param.7), kind=kOutput, calls=%fused_computation.17 | convolution fusion | flops 4299161088 | bytes 17827840 | tf_op jit(solution)/shard_map/dot_general | solution.py:15
  83.6 0.0 copy-start
  83.7 0.0 copy-done.3
  83.7 10.9 %multiply_reduce_fusion = (f32[512]{0:T(512)S(1)}, f32[512,4096]{1,0:T(8,128)S(1)}) fusion(f32[512,4096]{1,0:T(8,128)S(1)} %get-tuple-element.7, f32[512]{0:T(512)S(1)} %get-tuple-element.5, bf16[512,1024]{1,0:T(8,128)(2,1)S(1)} %copy-done.3, bf16[1,4096,1024]{2,1,0:T(8,128)(2,1)} %param.8), kind=kOutput, calls=%fused_computation.13 | convolution fusion | flops 4318035456 | bytes 26218496 | tf_op jit(solution)/shard_map/dot_general | solution.py:21
  94.6 0.0 copy-done
  94.6 3.5 subtract_convert_fusion
  98.1 0.0 copy-start.1
  98.1 1.9 copy-done.1
  100.1 6.7 %convolution_convert_fusion.5 = bf16[1024,4096]{1,0:T(8,128)(2,1)} fusion(bf16[512,1024]{1,0:T(8,128)(2,1)S(1)} %reshape.86, bf16[512,4096]{1,0:T(8,128)(2,1)S(1)} %subtract_convert_fusion), kind=kOutput, calls=%fused_computation.19 | convolution fusion | flops 4299161600 | bytes 13631488 | tf_op jit(solution)/shard_map/dot_general | solution.py:75
  106.8 0.0 reduce-scatter.3.cloned.1.call-update
  106.8 0.3 reduce-scatter.5.cloned.1.call-start
  107.1 12.4 %convolution_convert_fusion.4 = bf16[4096,1024]{1,0:T(8,128)(2,1)} fusion(bf16[512,1024]{1,0:T(8,128)(2,1)S(1)} %copy-done.3, f32[512,4096]{1,0:T(8,128)} %copy-done, f32[512]{0:T(512)S(1)} %get-tuple-element.5), kind=kOutput, calls=%fused_computation.18 | convolution fusion | flops 4311744512 | bytes 17827840 | tf_op jit(solution)/shard_map/dot_general | solution.py:84
  119.5 0.0 reduce-scatter.5.cloned.1.call-update
  119.5 9.2 %add_convert_fusion = bf16[512,1024]{1,0:T(8,128)(2,1)S(1)} fusion(bf16[512,1024]{1,0:T(8,128)(2,1)S(1)} %copy-done.3, bf16[512,4096]{1,0:T(8,128)(2,1)} %copy-done.1, bf16[1,1024,4096]{2,1,0:T(8,128)(2,1)} %param.7), kind=kOutput, calls=%fused_computation.22 | convolution fusion | flops 4296540160 | bytes 14680064 | tf_op jit(solution)/shard_map/dot_general | solution.py:27
  128.7 0.8 reshape.87
  129.4 3.0 collective-permute-start.1
  132.4 66.9 %collective-permute-done.1 = bf16[4,131072]{1,0:T(4,128)(2,1)S(1)} collective-permute-done((bf16[4,131072]{1,0:T(4,128)(2,1)S(1)}, bf16[4,131072]{1,0:T(4,128)(2,1)S(1)}, u32[]{:S(2)}, u32[]{:S(2)}) %collective-permute-start.1) | collective-permute-done | bytes 1048608 | tf_op jit(solution)/shard_map/ppermute | solution.py:11
  199.3 1.1 convolution_convert_fusion
  200.4 2.5 copy.10
  202.9 9.5 %all-to-all-start.1 = ((bf16[8,128,1024]{2,1,0:T(8,128)(2,1)}), bf16[8,128,1024]{2,1,0:T(8,128)(2,1)S(1)}, u32[]{:S(2)}, u32[]{:S(2)}) async-start(bf16[8,128,1024]{2,1,0:T(8,128)(2,1)} %copy.10), calls=%async_computation.1 | async-start | bytes 4194304 | tf_op jit(solution)/shard_map/all_to_all | solution.py:69
  212.4 11.4 %add_convert_fusion.1 = bf16[512,1024]{1,0:T(8,128)(2,1)} fusion(bf16[512,1024]{1,0:T(8,128)(2,1)S(1)} %reshape.86, bf16[1,4096,1024]{2,1,0:T(8,128)(2,1)} %param.8, f32[512,4096]{1,0:T(8,128)} %copy-done, f32[512]{0:T(512)S(1)} %get-tuple-element.5), kind=kOutput, calls=%fused_computation.23 | convolution fusion | flops 4309123072 | bytes 18876416 | tf_op jit(solution)/shard_map/dot_general | solution.py:19
  223.8 14.2 %all-to-all-done.1 = bf16[8,128,1024]{2,1,0:T(8,128)(2,1)S(1)} async-done(((bf16[8,128,1024]{2,1,0:T(8,128)(2,1)}), bf16[8,128,1024]{2,1,0:T(8,128)(2,1)S(1)}, u32[]{:S(2)}, u32[]{:S(2)}) %all-to-all-start.1) | async-done | bytes 2097184 | tf_op jit(solution)/shard_map/all_to_all | solution.py:69
  238.1 1.2 copy.12
  239.2 1.0 convolution_convert_fusion.3
  240.2 1.3 reshape.90
  241.5 68.9 %reduce-scatter.3.cloned.1.call-done = bf16[128,4096]{1,0:T(8,128)(2,1)} async-done(((bf16[1024,4096]{1,0:T(8,128)(2,1)}), bf16[128,4096]{1,0:T(8,128)(2,1)}) %reduce-scatter.3.cloned.1.call-update) | async-done | bytes 1048592 | tf_op jit(solution)/shard_map/reduce_scatter | solution.py:74
  310.4 2.4 fusion.12
  312.8 170.2 %reduce-scatter.5.cloned.1.call-done = bf16[512,1024]{1,0:T(8,128)(2,1)} async-done(((bf16[4096,1024]{1,0:T(8,128)(2,1)}), bf16[512,1024]{1,0:T(8,128)(2,1)}) %reduce-scatter.5.cloned.1.call-update) | async-done | bytes 1048592 | tf_op jit(solution)/shard_map/reduce_scatter | solution.py:83
  483.0 2.4 fusion.13
  (4 shorter events, 0.0 us)
Async XLA Ops:
  7.2 11.5 %copy-start.2 = (s32[1,2]{1,0:T(1,128)S(1)}, s32[1,2]{1,0:T(1,128)}, u32[]{:S(2)}) copy-start(s32[1,2]{1,0:T(1,128)} %param.6) | copy-start | bytes 28
  12.5 41.9 %all-to-all-start = ((bf16[8,128,1024]{2,1,0:T(8,128)(2,1)}), bf16[8,128,1024]{2,1,0:T(8,128)(2,1)S(1)}, u32[]{:S(2)}, u32[]{:S(2)}) async-start(bf16[8,128,1024]{2,1,0:T(8,128)(2,1)} %copy.9), calls=%async_computation | async-start | bytes 4194304 | tf_op jit(solution)/shard_map/all_to_all | solution.py:62
  18.7 291.7 %reduce-scatter.3.cloned.1.call-start = ((), (), s32[]{:S(2)}) async-start(), calls=%async_computation.4 | async-start | bytes 9437184 | tf_op jit(solution)/shard_map/reduce_scatter | solution.py:74
  56.2 19.3 %collective-permute-start = (bf16[4,131072]{1,0:T(4,128)(2,1)S(1)}, bf16[4,131072]{1,0:T(4,128)(2,1)S(1)}, u32[]{:S(2)}, u32[]{:S(2)}) collective-permute-start(bf16[4,131072]{1,0:T(4,128)(2,1)S(1)} %convolution_convert_fusion.2), channel_id=1, source_target_pairs={{0,8},{8,16},{16,24},{24,32},{32,40},{40,48},{48,56},{56,64},{64,7... | collective-permute-start | bytes 3145736 | tf_op jit(solution)/shard_map/ppermute | solution.py:11
  76.5 7.2 %copy-start.3 = (bf16[512,1024]{1,0:T(8,128)(2,1)S(1)}, bf16[512,1024]{1,0:T(8,128)(2,1)}, u32[]{:S(2)}) copy-start(bf16[512,1024]{1,0:T(8,128)(2,1)} %param.9) | copy-start | bytes 3145732
  83.6 11.0 %copy-start = (f32[512,4096]{1,0:T(8,128)}, f32[512,4096]{1,0:T(8,128)S(1)}, u32[]{:S(2)}) copy-start(f32[512,4096]{1,0:T(8,128)S(1)} %get-tuple-element.7) | copy-start | bytes 25165828
  98.1 2.0 copy-start.1
  106.8 376.2 %reduce-scatter.5.cloned.1.call-start = ((), (), s32[]{:S(2)}) async-start(), calls=%async_computation.5 | async-start | bytes 9437184 | tf_op jit(solution)/shard_map/reduce_scatter | solution.py:83
  129.4 69.9 %collective-permute-start.1 = (bf16[4,131072]{1,0:T(4,128)(2,1)S(1)}, bf16[4,131072]{1,0:T(4,128)(2,1)S(1)}, u32[]{:S(2)}, u32[]{:S(2)}) collective-permute-start(bf16[4,131072]{1,0:T(4,128)(2,1)S(1)} %reshape.87), channel_id=1, source_target_pairs={{0,120},{8,0},{16,8},{24,16},{32,24},{40,32},{48,40},{56,48},{64,5... | collective-permute-start | bytes 3145736 | tf_op jit(solution)/shard_map/ppermute | solution.py:11
  202.9 35.1 %all-to-all-start.1 = ((bf16[8,128,1024]{2,1,0:T(8,128)(2,1)}), bf16[8,128,1024]{2,1,0:T(8,128)(2,1)S(1)}, u32[]{:S(2)}, u32[]{:S(2)}) async-start(bf16[8,128,1024]{2,1,0:T(8,128)(2,1)} %copy.10), calls=%async_computation.1 | async-start | bytes 4194304 | tf_op jit(solution)/shard_map/all_to_all | solution.py:69
Sparse Core Ops, SparseCore 0:
  106.9 203.4 reduce-scatter.2
  312.8 170.1 reduce-scatter.4
where the time goes:
time: 493 us; the launch traced here: 492 us
  waiting for transfers between devices  332 us (67%)
  matrix products  61.9 us (13%)
  blocking collectives  35.2 us (7%)
  starting transfers between devices  26.5 us (5%)
  between operations  14.2 us (3%)
  local copies, waits for them, and re-layouts  13.7 us (3%)
  other arithmetic  8.73 us (2%)
    reduce_scatter x1, waiting for transfers between devices, shards(): lax.psum_scatter(lax.dot_general(part_rows, cotangent, contract, preferre...  170 us
    ppermute x2, waiting for transfers between devices, passed_along(): lax.ppermute(array, axis, [(i, (i + by) % devices) for i in range(devices)])  78.6 us
    reduce_scatter x1, waiting for transfers between devices, shards(): lax.psum_scatter(lax.dot_general(part_rows, dx, contract, preferred_eleme...  68.9 us
    all_gather x1, blocking collectives, shards(): table = lax.all_gather(routes, 'peer', axis=0, tiled=True)  35.2 us
    all_to_all x1, waiting for transfers between devices, shards(): lax.all_to_all(spread, 'peer', split_axis=0, concat_axis=0, tiled=True)  14.2 us
    dot_general x1, matrix products, shards(): lax.dot_general(part_rows, cotangent, contract, preferred_element_type=jn...  12.4 us
    dot_general x1, matrix products, layer(): y = jnp.dot(act, down_w, preferred_element_type=jnp.float32)  11.4 us
    dot_general x1, matrix products, layer(): lax.dot_general(cot, down_w, (((1,), (1,)), ((), ())), preferred_element_...  10.9 us
  transfers between devices with their start and end apart: 6, of which 5 were waited for; matrix products, arithmetic and copies ran while one was open for 9% of the time, Pallas kernels for 0%

commit v1 on v0

v1 whole, which is shorter than its diff:
```python
import functools

import jax
import jax.numpy as jnp
from jax import lax
from jax.experimental import pallas as pl
from jax.experimental.pallas import tpu as pltpu
from jax.sharding import PartitionSpec as P

eps = 1e-05
MESH = pl.DeviceIdType.MESH
f32 = jnp.float32
bf16 = jnp.bfloat16
ROWS_ROWS = (((0,), (0,)), ((), ()))
COLS_COLS = (((1,), (1,)), ((), ()))


def dot(a, b, dims=(((1,), (0,)), ((), ()))):
    return lax.dot_general(a, b, dims, preferred_element_type=f32)


def gates(x, r):
    z = x * r
    sig = 0.5 * jnp.tanh(0.5 * z) + 0.5
    act = z * sig
    slope = sig * (1.0 + z - act)
    return act, slope


def kernel(
    routes, codes, w_up, w_down, cot,
    out, grads, up_out, down_out,
    wu, wd, codes_all, cot_all, table_v, table_s, plan, live, stats,
    xbuf, x2buf, inp_own, inp3, cot2, yacc, down_acc, up_acc,
    out_v, up_v, down_v, ig_v,
    ssem, rsem, lsem,
):
    peers = lax.axis_size("peer")
    sections = lax.axis_size("section")
    slots = cot_all.shape[1]
    nblk = codes_all.shape[1]
    blk, width = codes_all.shape[2:]
    chunks, _, cols = wu.shape
    model = chunks * cols
    ring = peers // 2
    half = 2 * blk

    sec, me = lax.axis_index("section"), lax.axis_index("peer")
    nxt, prv = lax.rem(sec + 1, sections), lax.rem(sec + sections - 1, sections)
    xi, zi = me // 2, lax.rem(me, 2)
    zo = 1 - zi

    def at(dx, z):
        return 2 * lax.rem(xi + ring + dx, ring) + z

    zp, xr, xl, op = at(0, zo), at(1, zi), at(-1, zi), at(2, zi)
    xrz, xlz, opz = at(1, zo), at(-1, zo), at(2, zo)
    order = (me, zp, xl, xr, xlz, xrz, op, opz)

    barrier = pltpu.get_barrier_semaphore()
    for d in range(1, peers):
        pl.semaphore_signal(
            barrier, inc=1, device_id=(sec, lax.rem(me + d, peers)), device_id_type=MESH
        )
    for s in (nxt, prv):
        pl.semaphore_signal(barrier, inc=1, device_id=(s, me), device_id_type=MESH)

    def local(src, dst, i):
        c = pltpu.make_async_copy(src, dst, lsem.at[i])
        c.start()
        return c

    own_cot = [local(cot.at[pl.ds(k * blk, blk)], cot_all.at[me, k], k) for k in range(slots)]
    load_up = [
        local(w_up.at[:, pl.ds(c * cols, cols)], wu.at[c], slots + c) for c in range(chunks)
    ]
    load_down = [
        local(w_down.at[pl.ds(c * cols, cols)], wd.at[c], slots + chunks + c)
        for c in range(chunks)
    ]
    r0, r1 = routes[0, 0], routes[0, 1]
    lane = lax.broadcasted_iota(jnp.int32, (8, 128), 1)
    table_v[peers] = jnp.where(lane == 0, r0, r1)

    def remote(src, dst, i, s, p):
        return pltpu.make_async_remote_copy(
            src_ref=src, dst_ref=dst, send_sem=ssem.at[i], recv_sem=rsem.at[i],
            device_id=(s, p), device_id_type=MESH,
        )

    sent = []

    def send(src, dst, i, s, p):
        c = remote(src, dst, i, s, p)
        c.start()
        sent.append(c)

    def arrived(dst, i):
        remote(dst, dst, i, sec, zp).wait_recv()

    pieces = nblk + slots
    HOP = 7 * pieces
    ROUTE_HOP = HOP + nblk
    ROUTE = ROUTE_HOP + 1
    STAT = ROUTE + peers
    UPS = STAT + peers
    HOME = UPS + peers

    pl.semaphore_wait(barrier, peers + 1)

    send(table_v.at[peers], table_v.at[me], ROUTE_HOP, nxt, me)
    for b in range(nblk):
        send(codes.at[pl.ds(b * blk, blk)], codes_all.at[me, b], HOP + b, nxt, me)

    def chunk(g, owner):
        if g < nblk:
            return codes_all.at[owner, g]
        return cot_all.at[owner, g - nblk]

    def pass_on(g, owner, o, p):
        send(chunk(g, owner), chunk(g, owner), 7 * g + o - 1, sec, p)

    def start_own(g):
        pass_on(g, me, 1, zp)
        pass_on(g, me, 2, xr)
        pass_on(g, me, 3, xl)

    def wait_for(g, o):
        arrived(chunk(g, order[o]), 7 * g + o - 1)

    def pass_partner(g):
        wait_for(g, 1)
        pass_on(g, zp, 4, xr)
        pass_on(g, zp, 5, xl)

    def pass_opposite(g):
        if g % 2 == 0:
            wait_for(g, 2)
            pass_on(g, xl, 6, xr)
        else:
            wait_for(g, 3)
            pass_on(g, xr, 6, xl)

    def pass_across(g):
        wait_for(g, 6)
        pass_on(g, op, 7, zp)

    code_pieces = range(nblk)
    cot_pieces = range(nblk, pieces)

    for c in own_cot:
        c.wait()
    start_own(nblk)

    arrived(table_v.at[me], ROUTE_HOP)
    for d in range(1, peers):
        send(table_v.at[me], table_v.at[me], ROUTE + d, sec, lax.rem(me + d, peers))
    for g in code_pieces:
        arrived(codes_all.at[me, g], HOP + g)
        start_own(g)

    def codes_rows(j):
        return jnp.concatenate([codes_all[j, b] for b in range(nblk)], axis=0)

    for c in load_up:
        c.wait()

    def x2_step(c, carry):
        x2buf[c] = dot(codes_rows(me), wu[c])
        return carry

    lax.fori_loop(0, chunks // 2, x2_step, 0)
    for g in code_pieces:
        pass_partner(g)
    for g in code_pieces:
        pass_opposite(g)
    for g in list(cot_pieces)[1:]:
        start_own(g)
    lax.fori_loop(chunks // 2, chunks, x2_step, 0)

    for d in range(1, peers):
        j = lax.rem(me + d, peers)
        arrived(table_v.at[j], ROUTE + peers - d)
    fetch = local(table_v, table_s, 0)
    fetch.wait()

    def hits(p, q):
        first, second = table_s[p, 0, 0] == q, table_s[p, 0, 1] == q
        return (
            jnp.where(first | second, 1, 0),
            nblk * p + jnp.where(second, 1, 0),
        )

    def plan_step(q, carry):
        count = 0
        index = [0] * slots
        for p in range(peers):
            hit, block = hits(p, q)
            for k in range(slots):
                index[k] = jnp.where((hit == 1) & (count == k), block, index[k])
            count = count + hit
        for k in range(slots):
            plan[q * slots + k] = index[k]
            live[q * slots + k] = jnp.where(count > k, 1, 0)
        return carry

    lax.fori_loop(0, peers, plan_step, 0)

    def slot_codes(q, k):
        i = plan[q * slots + k]
        rows = codes_all[i // nblk, lax.rem(i, nblk)]
        return jnp.where(live[q * slots + k] == 1, rows, jnp.zeros_like(rows))

    for c in load_down:
        c.wait()
    for g in code_pieces:
        pass_across(g)
    for g in cot_pieces:
        pass_partner(g)
    for g in code_pieces:
        for o in (2, 3, 4, 5, 7):
            if not (o == 2 and g % 2 == 0) and not (o == 3 and g % 2 == 1):
                wait_for(g, o)

    eye = lax.broadcasted_iota(jnp.int32, (blk, blk), 0) == lax.broadcasted_iota(
        jnp.int32, (blk, blk), 1
    )

    def as_row(col):
        return jnp.sum(jnp.where(eye, col, 0.0), axis=0, keepdims=True)

    def as_col(row):
        return jnp.sum(jnp.where(eye, row, 0.0), axis=1, keepdims=True)

    saves = []
    rows_r, rows_c = [], []
    for h in range(slots // 2):
        for j in range(2):
            inp_own[pl.ds(j * blk, blk)] = slot_codes(me, 2 * h + j)

        def x_step(c, ssq):
            x = dot(inp_own[...], wu[c])
            xbuf[c] = x
            return ssq + jnp.sum(x * x, axis=-1, keepdims=True)

        ssq = lax.fori_loop(0, chunks, x_step, jnp.zeros((half, 1), f32))
        r = lax.rsqrt(ssq * (1.0 / model) + eps)
        if h == 0:
            for g in list(cot_pieces)[:2]:
                pass_opposite(g)
        else:
            for g in list(cot_pieces)[:2]:
                pass_across(g)
        yacc[...] = jnp.zeros_like(yacc)
        cot_h = jnp.concatenate([cot_all[me, 2 * h], cot_all[me, 2 * h + 1]], axis=0)

        def y_step(c, m):
            x = xbuf[c]
            act, slope = gates(x, r)
            yacc[...] += dot(act.astype(bf16), wd[c])
            back = dot(cot_h, wd[c], COLS_COLS)
            return m + jnp.sum(x * (back * slope), axis=-1, keepdims=True)

        m = lax.fori_loop(0, chunks, y_step, jnp.zeros((half, 1), f32)) * (1.0 / model)
        if h == 0:
            for g in list(cot_pieces)[2:]:
                pass_opposite(g)
        c3 = (r * r * r) * m
        for j in range(2):
            rows_r.append(as_row(r[j * blk : (j + 1) * blk]))
            rows_c.append(as_row(c3[j * blk : (j + 1) * blk]))
        out_v[pl.ds(h * half, half)] = (inp_own[...].astype(f32) + yacc[...]).astype(bf16)
        saves.append(local(out_v.at[pl.ds(h * half, half)], out.at[pl.ds(h * half, half)], 1 + h))
    stats[me] = jnp.concatenate(rows_r + rows_c, axis=0)
    for d in range(1, peers):
        send(stats.at[me], stats.at[me], STAT + d, sec, lax.rem(me + d, peers))
    for g in list(cot_pieces)[2:]:
        pass_across(g)
    for d in range(1, peers):
        j = lax.rem(me + d, peers)
        arrived(stats.at[j], STAT + peers - d)

    down_acc[...] = jnp.zeros_like(down_acc)
    up_acc[...] = jnp.zeros_like(up_acc)

    def all_slots(q):
        for k in range(slots):
            inp3[pl.ds(k * blk, blk)] = slot_codes(q, k)
        tile = stats[q]
        r = jnp.concatenate([as_col(tile[k : k + 1]) for k in range(slots)], axis=0)
        c3 = jnp.concatenate([as_col(tile[slots + k : slots + k + 1]) for k in range(slots)], axis=0)
        cot_q = jnp.concatenate([cot_all[q, k] for k in range(slots)], axis=0)
        x = dot(inp3[...], wu[me])
        act, slope = gates(x, r)
        down_acc[...] += dot(act.astype(bf16), cot_q, ROWS_ROWS)
        back = dot(cot_q, wd[me], COLS_COLS)
        dx = (r * (back * slope) - x * c3).astype(bf16)
        up_acc[...] += dot(inp3[...], dx, ROWS_ROWS)

    def owner_of(o):
        q = order[0]
        for n in range(1, peers):
            q = jnp.where(o == n, order[n], q)
        return q

    def owner_step(o, carry):
        all_slots(owner_of(o))
        return carry

    lax.fori_loop(0, 2, owner_step, 0)
    for g in cot_pieces:
        for o in (2, 3, 4, 5, 7):
            if not (o == 2 and g % 2 == 0) and not (o == 3 and g % 2 == 1):
                wait_for(g, o)
    lax.fori_loop(2, peers, owner_step, 0)

    factor = 1.0 / (peers * nblk)
    tall = width // peers
    up_v[...] = (up_acc[...] * factor).astype(bf16)
    for d in range(1, peers):
        j = lax.rem(me + d, peers)
        send(
            up_v.at[pl.ds(pl.multiple_of(j * tall, tall), tall)],
            up_out.at[:, pl.ds(pl.multiple_of(me * cols, cols), cols)],
            UPS + d, sec, j,
        )
    saves.append(local(
        up_v.at[pl.ds(pl.multiple_of(me * tall, tall), tall)],
        up_out.at[:, pl.ds(pl.multiple_of(me * cols, cols), cols)], 3,
    ))
    down_v[...] = (down_acc[...] * factor).astype(bf16)
    saves.append(local(down_v, down_out, 4))

    r2, c2 = [], []
    for b in range(nblk):
        q = table_s[me, 0, b]
        k = 0
        for p in range(peers):
            hit, _ = hits(p, q)
            k = k + jnp.where(p < me, hit, 0)
        k = jnp.minimum(k, slots - 1)
        cot2[pl.ds(b * blk, blk)] = cot_all[q, k]
        tile = stats[q]
        sub = lax.broadcasted_iota(jnp.int32, tile.shape, 0)
        r2.append(as_col(jnp.sum(jnp.where(sub == k, tile, 0.0), axis=0, keepdims=True)))
        c2.append(as_col(jnp.sum(jnp.where(sub == slots + k, tile, 0.0), axis=0, keepdims=True)))
    r2, c2 = jnp.concatenate(r2, axis=0), jnp.concatenate(c2, axis=0)
    yacc[...] = cot2[...].astype(f32)

    def home_step(c, carry):
        x = x2buf[c]
        _, slope = gates(x, r2)
        back = dot(cot2[...], wd[c], COLS_COLS)
        dx = (r2 * (back * slope) - x * c2).astype(bf16)
        yacc[...] += dot(dx, wu[c], COLS_COLS)
        return carry

    lax.fori_loop(0, chunks, home_step, 0)
    ig_v[...] = yacc[...].astype(bf16)
    send(ig_v, grads, HOME, prv, me)

    for c in saves:
        c.wait()
    for d in range(1, peers):
        j = lax.rem(me + peers - d, peers)
        arrived(up_out.at[:, pl.ds(pl.multiple_of(j * cols, cols), cols)], UPS + d)
    arrived(grads, HOME)
    for c in sent:
        c.wait_send()


def shards(codes, routes, w_up, w_down, cotangent):
    peers = lax.axis_size("peer")
    nblk = routes.shape[1]
    rows, width = codes.shape
    blk = rows // nblk
    slots = cotangent.shape[0] // blk
    model = w_up.shape[2]
    cols = model // peers
    half = 2 * blk
    anywhere = pl.BlockSpec(memory_space=pl.ANY)
    copies = 7 * (nblk + slots) + nblk + 2 + 3 * peers
    out, grads, up, down = pl.pallas_call(
        kernel,
        out_shape=(
            jax.ShapeDtypeStruct((slots * blk, width), bf16),
            jax.ShapeDtypeStruct((rows, width), bf16),
            jax.ShapeDtypeStruct((width // peers, model), bf16),
            jax.ShapeDtypeStruct((cols, width), bf16),
        ),
        in_specs=[pl.BlockSpec(memory_space=pltpu.SMEM)] + [anywhere] * 4,
        out_specs=[anywhere] * 4,
        scratch_shapes=[
            pltpu.VMEM((peers, width, cols), bf16),
            pltpu.VMEM((peers, cols, width), bf16),
            pltpu.VMEM((peers, nblk, blk, width), bf16),
            pltpu.VMEM((peers, slots, blk, width), bf16),
            pltpu.VMEM((peers + 1, 8, 128), jnp.int32),
            pltpu.SMEM((peers + 1, 8, 128), jnp.int32),
            pltpu.SMEM((peers * slots,), jnp.int32),
            pltpu.SMEM((peers * slots,), jnp.int32),
            pltpu.VMEM((peers, 2 * slots, blk), f32),
            pltpu.VMEM((peers, half, cols), f32),
            pltpu.VMEM((peers, rows, cols), f32),
            pltpu.VMEM((half, width), bf16),
            pltpu.VMEM((slots * blk, width), bf16),
            pltpu.VMEM((rows, width), bf16),
            pltpu.VMEM((half, width), f32),
            pltpu.VMEM((cols, width), f32),
            pltpu.VMEM((width, cols), f32),
            pltpu.VMEM((slots * blk, width), bf16),
            pltpu.VMEM((width, cols), bf16),
            pltpu.VMEM((cols, width), bf16),
            pltpu.VMEM((rows, width), bf16),
            pltpu.SemaphoreType.DMA((copies,)),
            pltpu.SemaphoreType.DMA((copies,)),
            pltpu.SemaphoreType.DMA((slots + 2 * peers,)),
        ],
        compiler_params=pltpu.CompilerParams(
            collective_id=0, has_side_effects=True, vmem_limit_bytes=60 * 1024 * 1024,
        ),
        name="relay",
    )(routes, codes, w_up[0], w_down[0], cotangent)
    return out, grads, up[None], down[None]


def solution(mesh):
    placed = (
        P(("section", "peer"), None),
        P(("section", "peer"), None),
        P("section", None, None),
        P("section", None, None),
        P(("section", "peer"), None),
    )
    return jax.shard_map(
        shards,
        mesh=mesh,
        in_specs=placed,
        out_specs=(
            P(("section", "peer"), None),
            P(("section", "peer"), None),
            P("section", "peer", None),
            P("section", "peer", None),
        ),
        check_vma=False,
    )
```

time: 493 us -> 161 us (0.33)
  waiting for transfers between devices: 332 us -> 0 us
  Pallas kernels: 0 us -> 149 us
  matrix products: 61.9 us -> 0 us
  blocking collectives: 35.2 us -> 0 us
  starting transfers between devices: 26.5 us -> 0 us
  between operations: 14.2 us -> 0.64 us
  other arithmetic: 8.73 us -> 0 us
  local copies, waits for them, and re-layouts: 13.7 us -> 8.68 us
    reduce_scatter x2 -> x0, waiting for transfers between devices: 239 us -> none  [the longest x1 170 us: shards(): lax.psum_scatter(lax.dot_general(part_rows, cotangent, contract, preferre...]
    pallas_call x0 -> x1, Pallas kernels: none -> 149 us  [shards(): pl.pallas_call(kernel, out_shape=(jax.ShapeDtypeStruct((slots * blk, widt...]
    ppermute x2 -> x0, waiting for transfers between devices: 78.6 us -> none  [passed_along(): lax.ppermute(array, axis, [(i, (i + by) % devices) for i in range(devices)])]
    dot_general x10 -> x0, matrix products: 61.9 us -> none  [the longest x1 12.4 us: shards(): lax.dot_general(part_rows, cotangent, contract, preferred_element_type=jn...]
    all_gather x1 -> x0, blocking collectives: 35.2 us -> none  [shards(): table = lax.all_gather(routes, 'peer', axis=0, tiled=True)]
    all_to_all x2 -> x0, starting transfers between devices: 15.7 us -> none  [the longest x1 9.47 us: shards(): lax.all_to_all(spread, 'peer', split_axis=0, concat_axis=0, tiled=True)]
    all_to_all x2 -> x0, waiting for transfers between devices: 14.2 us -> none  [the longest x1 14.2 us: shards(): lax.all_to_all(spread, 'peer', split_axis=0, concat_axis=0, tiled=True)]
    ppermute x2 -> x0, starting transfers between devices: 10.6 us -> none  [passed_along(): lax.ppermute(array, axis, [(i, (i + by) % devices) for i in range(devices)])]
  transfers between devices with their start and end apart: 6 -> 0, of which waited for: 5 -> 0; matrix products, arithmetic and copies ran while one was open for 9% -> 0% of each run, Pallas kernels for 0% -> 0%
where the time goes in v1:
time: 161 us; the launch traced here: 158 us
  Pallas kernels  149 us (93%)
  local copies, waits for them, and re-layouts  8.68 us (5%)
    pallas_call x1, Pallas kernels, shards(): pl.pallas_call(kernel, out_shape=(jax.ShapeDtypeStruct((slots * blk, widt...  149 us
    unnamed x4, local copies, waits for them, and re-layouts  8.68 us

profile of v1, /device:TPU:1, one launch (start us, length us, event | category | flops | bytes accessed | tf_op | source)
XLA Modules:
  0.0 158.1 jit_solution(6614608383215681630)
XLA Ops:
  0.6 148.7 %relay.1 = (bf16[512,1024]{1,0:T(8,128)(2,1)}, bf16[256,1024]{1,0:T(8,128)(2,1)}, bf16[128,4096]{1,0:T(8,128)(2,1)}, bf16[512,1024]{1,0:T(8,128)(2,1)}) custom-call(s32[1,2]{1,0:T(1,128)} %routes.1, bf16[256,1024]{1,0:T(8,128)(2,1)} %codes.1, bf16[1024,4096]{1,0:T(8,128)(2,1)} %bitcast.4, bf16[4096,1024]{1,0:T(8,128)(2,1)} %bitcast.5, bf16[512,1024]{1,0:T(8,128)(2,1)} %cot.1), custom_call_target="tpu_custom_call" | custom-call | tf_op jit(solution)/shard_map/relay/pallas_call | solution.py:383
  149.4 2.3 %copy.13 = bf16[512,1024]{1,0:T(8,128)(2,1)} copy(bf16[512,1024]{1,0:T(8,128)(2,1)} %get-tuple-element.16) | data formatting | bytes 2097152
  151.6 1.9 %copy.14 = bf16[256,1024]{1,0:T(8,128)(2,1)} copy(bf16[256,1024]{1,0:T(8,128)(2,1)} %get-tuple-element.17) | data formatting | bytes 1048576
  153.5 2.3 %copy.15 = bf16[1,128,4096]{2,1,0:T(8,128)(2,1)} copy(bf16[1,128,4096]{2,1,0:T(8,128)(2,1)} %bitcast.7) | data formatting | bytes 2097152
  155.8 2.3 %copy.16 = bf16[1,512,1024]{2,1,0:T(8,128)(2,1)} copy(bf16[1,512,1024]{2,1,0:T(8,128)(2,1)} %bitcast.6) | data formatting | bytes 2097152

commit v2 on v1

v2 whole, which is shorter than its diff:
```python
import functools

import jax
import jax.numpy as jnp
from jax import lax
from jax.experimental import pallas as pl
from jax.experimental.pallas import tpu as pltpu
from jax.sharding import PartitionSpec as P

eps = 1e-05
MESH = pl.DeviceIdType.MESH
f32 = jnp.float32
bf16 = jnp.bfloat16
ROWS_ROWS = (((0,), (0,)), ((), ()))
COLS_COLS = (((1,), (1,)), ((), ()))


def dot(a, b, dims=(((1,), (0,)), ((), ()))):
    return lax.dot_general(a, b, dims, preferred_element_type=f32)


def gates(x, r):
    z = x * r
    sig = 0.5 * jnp.tanh(0.5 * z) + 0.5
    act = z * sig
    slope = sig * (1.0 + z - act)
    return act, slope


def kernel(
    routes, codes, w_up, w_down, cot,
    out, grads, up_out, down_out,
    wu, wd, codes_all, cot_own, cot_all, table_v, table_s, plan, live, base, packed, stats,
    xbuf, x2buf, bbuf, inp_own, inp3, cot3, yacc, move, land,
    out_v, up_v, down_v, ig_v,
    ssem, rsem, lsem,
):
    peers = lax.axis_size("peer")
    sections = lax.axis_size("section")
    slots = cot_own.shape[0]
    nblk = codes_all.shape[1]
    blk, width = codes_all.shape[2:]
    chunks, _, cols = wu.shape
    model = chunks * cols
    ring = peers // 2
    half = 2 * blk
    low, high = pl.ds(0, blk // 2), pl.ds(blk // 2, blk // 2)

    sec, me = lax.axis_index("section"), lax.axis_index("peer")
    nxt, prv = lax.rem(sec + 1, sections), lax.rem(sec + sections - 1, sections)
    xi, zi = me // 2, lax.rem(me, 2)
    zo = 1 - zi

    def at(dx, z):
        return 2 * lax.rem(xi + ring + dx, ring) + z

    zp, xr, xl, op = at(0, zo), at(1, zi), at(-1, zi), at(2, zi)
    xrz, xlz, opz = at(1, zo), at(-1, zo), at(2, zo)
    order = (me, zp, xl, xr, xlz, xrz, op, opz)

    barrier = pltpu.get_barrier_semaphore()
    for d in range(1, peers):
        pl.semaphore_signal(
            barrier, inc=1, device_id=(sec, lax.rem(me + d, peers)), device_id_type=MESH
        )
    for s in (nxt, prv):
        pl.semaphore_signal(barrier, inc=1, device_id=(s, me), device_id_type=MESH)

    def local(src, dst, i):
        c = pltpu.make_async_copy(src, dst, lsem.at[i])
        c.start()
        return c

    load_first = local(cot.at[pl.ds(0, blk)], cot_all.at[0, me], slots)
    load_cot = [local(cot.at[pl.ds(k * blk, blk)], cot_own.at[k], k) for k in range(slots)]
    load_up = [
        local(w_up.at[:, pl.ds(c * cols, cols)], wu.at[c], slots + 1 + c) for c in range(chunks)
    ]
    load_down = [
        local(w_down.at[pl.ds(c * cols, cols)], wd.at[c], slots + 1 + chunks + c)
        for c in range(chunks)
    ]
    r0, r1 = routes[0, 0], routes[0, 1]
    lane = lax.broadcasted_iota(jnp.int32, (8, 128), 1)
    table_v[peers] = jnp.where(lane == 0, r0, r1)

    def remote(src, dst, i, s, p):
        return pltpu.make_async_remote_copy(
            src_ref=src, dst_ref=dst, send_sem=ssem.at[i], recv_sem=rsem.at[i],
            device_id=(s, p), device_id_type=MESH,
        )

    sent = []

    def send(src, dst, i, s, p):
        c = remote(src, dst, i, s, p)
        c.start()
        sent.append(c)

    def arrived(dst, i):
        remote(dst, dst, i, sec, zp).wait_recv()

    FIRST, MORE = nblk, nblk + 1
    pieces = nblk + 2
    HOP = 7 * pieces
    ROUTE_HOP = HOP + nblk
    ROUTE = ROUTE_HOP + 1
    STAT = ROUTE + peers
    UPS = STAT + peers
    HOME = UPS + peers
    PACK = HOME + 1

    pl.semaphore_wait(barrier, peers + 1)

    send(table_v.at[peers], table_v.at[me], ROUTE_HOP, nxt, me)
    for b in range(nblk):
        send(codes.at[pl.ds(b * blk, blk)], codes_all.at[me, b], HOP + b, nxt, me)

    def chunk(g, owner):
        if g < nblk:
            return codes_all.at[owner, g]
        return cot_all.at[g - nblk, owner]

    def pass_on(g, owner, o, p):
        send(chunk(g, owner), chunk(g, owner), 7 * g + o - 1, sec, p)

    def start_own(g):
        pass_on(g, me, 1, zp)
        pass_on(g, me, 2, xr)
        pass_on(g, me, 3, xl)

    def wait_for(g, o):
        arrived(chunk(g, order[o]), 7 * g + o - 1)

    def pass_partner(g):
        wait_for(g, 1)
        pass_on(g, zp, 4, xr)
        pass_on(g, zp, 5, xl)

    def pass_opposite(g):
        if g % 2 == 0:
            wait_for(g, 2)
            pass_on(g, xl, 6, xr)
        else:
            wait_for(g, 3)
            pass_on(g, xr, 6, xl)

    def pass_across(g):
        wait_for(g, 6)
        pass_on(g, op, 7, zp)

    def wait_rest(g):
        for o in (3 if g % 2 == 0 else 2, 4, 5, 7):
            wait_for(g, o)

    load_first.wait()
    start_own(FIRST)

    arrived(table_v.at[me], ROUTE_HOP)
    for d in range(1, peers):
        send(table_v.at[me], table_v.at[me], ROUTE + d, sec, lax.rem(me + d, peers))
    for g in range(nblk):
        arrived(codes_all.at[me, g], HOP + g)
        start_own(g)

    for d in range(1, peers):
        j = lax.rem(me + d, peers)
        arrived(table_v.at[j], ROUTE + peers - d)
    fetch = local(table_v, table_s, slots)
    fetch.wait()

    def hits(p, q):
        first, second = table_s[p, 0, 0] == q, table_s[p, 0, 1] == q
        return (
            jnp.where(first | second, 1, 0),
            nblk * p + jnp.where(second, 1, 0),
        )

    def plan_step(q, before):
        count = 0
        index = [0] * slots
        for p in range(peers):
            hit, block = hits(p, q)
            for k in range(slots):
                index[k] = jnp.where((hit == 1) & (count == k), block, index[k])
            count = count + hit
        for k in range(slots):
            plan[q * slots + k] = index[k]
            live[q * slots + k] = jnp.where(count > k, 1, 0)
        base[q] = before
        return before + count - 1

    lax.fori_loop(0, peers, plan_step, 0)

    def packed_at(q, k):
        return jnp.where(live[q * slots + k] == 1, base[q] + k - 1, -1)

    for c in load_cot:
        c.wait()

    def mine(j):
        rows = jnp.zeros((blk, width), bf16)
        for k in range(1, slots):
            rows = jnp.where(packed_at(me, k) == j, cot_own[k], rows)
        return rows

    move[0] = mine(opz)
    send(move.at[0], land.at[0], PACK + 0, sec, zp)
    move[5] = mine(xrz)
    send(move.at[5], land.at[5], PACK + 5, sec, xr)
    move[6] = mine(xlz)
    send(move.at[6], land.at[6], PACK + 6, sec, xl)

    def codes_rows(j):
        return jnp.concatenate([codes_all[j, b] for b in range(nblk)], axis=0)

    for c in load_up:
        c.wait()

    def x2_step(c, carry):
        x2buf[c] = dot(codes_rows(me), wu[c])
        return carry

    lax.fori_loop(0, chunks // 2, x2_step, 0)
    for g in range(nblk):
        pass_partner(g)
    arrived(land.at[0], PACK + 0)
    move[1] = mine(op) + land[0]
    send(move.at[1, low], land.at[1, low], PACK + 1, sec, xr)
    send(move.at[1, high], land.at[1, high], PACK + 2, sec, xl)
    for g in range(nblk):
        pass_opposite(g)
    lax.fori_loop(chunks // 2, chunks, x2_step, 0)
    arrived(land.at[1, low], PACK + 1)
    arrived(land.at[1, high], PACK + 2)
    move[3] = mine(xr)
    move[3, low] = move[3, low] + land[1, low]
    send(move.at[3], land.at[3], PACK + 3, sec, xr)
    move[4] = mine(xl)
    move[4, high] = move[4, high] + land[1, high]
    send(move.at[4], land.at[4], PACK + 4, sec, xl)
    arrived(land.at[5], PACK + 5)
    arrived(land.at[6], PACK + 6)
    move[2] = mine(zp) + land[5] + land[6]
    send(move.at[2], land.at[2], PACK + 7, sec, zp)
    pass_partner(FIRST)

    for c in load_down:
        c.wait()

    def back_step(c, carry):
        rows = jnp.concatenate([cot_own[k] for k in range(slots)], axis=0)
        bbuf[c] = dot(rows, wd[c], COLS_COLS)
        return carry

    lax.fori_loop(0, chunks // 2, back_step, 0)
    for g in range(nblk):
        pass_across(g)
    arrived(land.at[3], PACK + 3)
    arrived(land.at[4], PACK + 4)
    arrived(land.at[2], PACK + 7)
    cot_all[1, me] = mine(me) + land[3] + land[4] + land[2]
    start_own(MORE)
    pass_opposite(FIRST)
    lax.fori_loop(chunks // 2, chunks, back_step, 0)
    for g in range(nblk):
        wait_rest(g)

    eye = lax.broadcasted_iota(jnp.int32, (blk, blk), 0) == lax.broadcasted_iota(
        jnp.int32, (blk, blk), 1
    )

    def as_row(col):
        return jnp.sum(jnp.where(eye, col, 0.0), axis=0, keepdims=True)

    def as_col(row):
        return jnp.sum(jnp.where(eye, row, 0.0), axis=1, keepdims=True)

    def block_codes(i):
        return codes_all[i // nblk, lax.rem(i, nblk)]

    def slot_codes(q, k):
        rows = block_codes(plan[q * slots + k])
        return jnp.where(live[q * slots + k] == 1, rows, jnp.zeros_like(rows))

    saves = []
    rows_r, rows_c = [], []
    for h in range(slots // 2):
        for j in range(2):
            inp_own[pl.ds(j * blk, blk)] = slot_codes(me, 2 * h + j)

        def x_step(c, ssq):
            x = dot(inp_own[...], wu[c])
            xbuf[c] = x
            return ssq + jnp.sum(x * x, axis=-1, keepdims=True)

        ssq = lax.fori_loop(0, chunks, x_step, jnp.zeros((half, 1), f32))
        r = lax.rsqrt(ssq * (1.0 / model) + eps)
        if h == 0:
            pass_partner(MORE)
            pass_across(FIRST)
        else:
            pass_across(MORE)
        yacc[...] = jnp.zeros_like(yacc)

        def y_step(c, m):
            x = xbuf[c]
            act, slope = gates(x, r)
            yacc[...] += dot(act.astype(bf16), wd[c])
            back = bbuf[c, pl.ds(h * half, half)]
            return m + jnp.sum(x * (back * slope), axis=-1, keepdims=True)

        m = lax.fori_loop(0, chunks, y_step, jnp.zeros((half, 1), f32)) * (1.0 / model)
        if h == 0:
            pass_opposite(MORE)
        c3 = (r * r * r) * m
        for j in range(2):
            rows_r.append(as_row(r[j * blk : (j + 1) * blk]))
            rows_c.append(as_row(c3[j * blk : (j + 1) * blk]))
        out_v[pl.ds(h * half, half)] = (inp_own[...].astype(f32) + yacc[...]).astype(bf16)
        saves.append(local(out_v.at[pl.ds(h * half, half)], out.at[pl.ds(h * half, half)], h))
    stats[me] = jnp.concatenate(rows_r + rows_c, axis=0)
    for d in range(1, peers):
        send(stats.at[me], stats.at[me], STAT + d, sec, lax.rem(me + d, peers))

    def packed_step(j, carry):
        block, peer, slot = 0, 0, 1
        for q in range(peers):
            for k in range(1, slots):
                hit = packed_at(q, k) == j
                block = jnp.where(hit, plan[q * slots + k], block)
                peer = jnp.where(hit, q, peer)
                slot = jnp.where(hit, k, slot)
        packed[3 * j], packed[3 * j + 1], packed[3 * j + 2] = block, peer, slot
        return carry

    lax.fori_loop(0, peers, packed_step, 0)
    wait_rest(FIRST)
    for d in range(1, peers):
        j = lax.rem(me + d, peers)
        arrived(stats.at[j], STAT + peers - d)

    def row_values(q, k):
        tile = stats[q]
        sub = lax.broadcasted_iota(jnp.int32, tile.shape, 0)
        return [
            as_col(jnp.sum(jnp.where(sub == n, tile, 0.0), axis=0, keepdims=True))
            for n in (k, slots + k)
        ]

    parts = width // cols
    sums = pl.ds(0, cols)
    for n in range(2 * parts):
        bbuf[n, sums] = jnp.zeros((cols, cols), f32)

    def four(blocks):
        rs, cs = [], []
        for n, (rows, cots, q, k) in enumerate(blocks):
            inp3[pl.ds(n * blk, blk)] = rows
            cot3[pl.ds(n * blk, blk)] = cots
            r, c3 = row_values(q, k)
            rs.append(r)
            cs.append(c3)
        r, c3 = jnp.concatenate(rs, axis=0), jnp.concatenate(cs, axis=0)
        x = dot(inp3[...], wu[me])
        act, slope = gates(x, r)
        act = act.astype(bf16)
        back = dot(cot3[...], wd[me], COLS_COLS)
        dx = (r * (back * slope) - x * c3).astype(bf16)
        for n in range(parts):
            bbuf[n, sums] += dot(inp3[:, pl.ds(n * cols, cols)], dx, ROWS_ROWS)
            bbuf[parts + n, sums] += dot(act, cot3[:, pl.ds(n * cols, cols)], ROWS_ROWS)

    def first_step(i, carry):
        blocks = []
        for n in range(4):
            q = 4 * i + n
            blocks.append((block_codes(plan[q * slots]), cot_all[0, q], q, 0))
        four(blocks)
        return carry

    def more_step(i, carry):
        blocks = []
        for n in range(4):
            j = 4 * i + n
            block, q, k = packed[3 * j], packed[3 * j + 1], packed[3 * j + 2]
            blocks.append((block_codes(block), cot_all[1, j], q, k))
        four(blocks)
        return carry

    lax.fori_loop(0, peers // 4, first_step, 0)
    wait_rest(MORE)
    lax.fori_loop(0, peers // 4, more_step, 0)

    factor = 1.0 / (peers * nblk)
    tall = width // peers
    for n in range(parts):
        up_v[pl.ds(n * cols, cols)] = (bbuf[n, sums] * factor).astype(bf16)
    for d in range(1, peers):
        j = lax.rem(me + d, peers)
        send(
            up_v.at[pl.ds(pl.multiple_of(j * tall, tall), tall)],
            up_out.at[:, pl.ds(pl.multiple_of(me * cols, cols), cols)],
            UPS + d, sec, j,
        )
    saves.append(local(
        up_v.at[pl.ds(pl.multiple_of(me * tall, tall), tall)],
        up_out.at[:, pl.ds(pl.multiple_of(me * cols, cols), cols)], 2,
    ))
    for n in range(parts):
        down_v[:, pl.ds(n * cols, cols)] = (bbuf[parts + n, sums] * factor).astype(bf16)
    saves.append(local(down_v, down_out, 3))

    r2, c2 = [], []
    for b in range(nblk):
        q = table_s[me, 0, b]
        k = 0
        for p in range(peers):
            hit, _ = hits(p, q)
            k = k + jnp.where(p < me, hit, 0)
        k = jnp.minimum(k, slots - 1)
        j = jnp.clip(base[q] + k - 1, 0, peers - 1)
        cot3[pl.ds(b * blk, blk)] = jnp.where(k == 0, cot_all[0, q], cot_all[1, j])
        r, c3 = row_values(q, k)
        r2.append(r)
        c2.append(c3)
    r2, c2 = jnp.concatenate(r2, axis=0), jnp.concatenate(c2, axis=0)
    two = pl.ds(0, nblk * blk)
    yacc[...] = cot3[two].astype(f32)

    def home_step(c, carry):
        x = x2buf[c]
        _, slope = gates(x, r2)
        back = dot(cot3[two], wd[c], COLS_COLS)
        dx = (r2 * (back * slope) - x * c2).astype(bf16)
        yacc[...] += dot(dx, wu[c], COLS_COLS)
        return carry

    lax.fori_loop(0, chunks, home_step, 0)
    ig_v[...] = yacc[...].astype(bf16)
    send(ig_v, grads, HOME, prv, me)

    for c in saves:
        c.wait()
    for d in range(1, peers):
        j = lax.rem(me + peers - d, peers)
        arrived(up_out.at[:, pl.ds(pl.multiple_of(j * cols, cols), cols)], UPS + d)
    arrived(grads, HOME)
    for c in sent:
        c.wait_send()


def copy_kernel(*refs):
    n = (len(refs) - 2) // 3
    sources, results, held = refs[:n], refs[n : 2 * n], refs[2 * n : 3 * n]
    in_sem, out_sem = refs[3 * n :]
    loads = []
    for src, mid in zip(sources, held):
        rows = src.shape[0] // 4
        for k in range(4):
            part = pl.ds(k * rows, rows)
            loads.append(pltpu.make_async_copy(src.at[part], mid.at[part], in_sem.at[len(loads)]))
    for c in loads:
        c.start()
    stores = []
    for mid, dst in zip(held, results):
        rows = dst.shape[0] // 4
        for k in range(4):
            part = pl.ds(k * rows, rows)
            loads[len(stores)].wait()
            c = pltpu.make_async_copy(mid.at[part], dst.at[part], out_sem.at[len(stores)])
            c.start()
            stores.append(c)
    for c in stores:
        c.wait()


def shards(codes, routes, w_up, w_down, cotangent):
    peers = lax.axis_size("peer")
    nblk = routes.shape[1]
    rows, width = codes.shape
    blk = rows // nblk
    slots = cotangent.shape[0] // blk
    model = w_up.shape[2]
    cols = model // peers
    half = 2 * blk
    anywhere = pl.BlockSpec(memory_space=pl.ANY)
    copies = 7 * (nblk + 2) + nblk + 2 + 3 * peers + 8
    shapes = (
        jax.ShapeDtypeStruct((slots * blk, width), bf16),
        jax.ShapeDtypeStruct((rows, width), bf16),
        jax.ShapeDtypeStruct((width // peers, model), bf16),
        jax.ShapeDtypeStruct((cols, width), bf16),
    )
    results = pl.pallas_call(
        kernel,
        out_shape=shapes,
        in_specs=[pl.BlockSpec(memory_space=pltpu.SMEM)] + [anywhere] * 4,
        out_specs=[anywhere] * 4,
        scratch_shapes=[
            pltpu.VMEM((peers, width, cols), bf16),
            pltpu.VMEM((peers, cols, width), bf16),
            pltpu.VMEM((peers, nblk, blk, width), bf16),
            pltpu.VMEM((slots, blk, width), bf16),
            pltpu.VMEM((2, peers, blk, width), bf16),
            pltpu.VMEM((peers + 1, 8, 128), jnp.int32),
            pltpu.SMEM((peers + 1, 8, 128), jnp.int32),
            pltpu.SMEM((peers * slots,), jnp.int32),
            pltpu.SMEM((peers * slots,), jnp.int32),
            pltpu.SMEM((peers,), jnp.int32),
            pltpu.SMEM((3 * peers,), jnp.int32),
            pltpu.VMEM((peers, 2 * slots, blk), f32),
            pltpu.VMEM((peers, half, cols), f32),
            pltpu.VMEM((peers, rows, cols), f32),
            pltpu.VMEM((peers, slots * blk, cols), f32),
            pltpu.VMEM((half, width), bf16),
            pltpu.VMEM((slots * blk, width), bf16),
            pltpu.VMEM((slots * blk, width), bf16),
            pltpu.VMEM((half, width), f32),
            pltpu.VMEM((7, blk, width), bf16),
            pltpu.VMEM((7, blk, width), bf16),
            pltpu.VMEM((slots * blk, width), bf16),
            pltpu.VMEM((width, cols), bf16),
            pltpu.VMEM((cols, width), bf16),
            pltpu.VMEM((rows, width), bf16),
            pltpu.SemaphoreType.DMA((copies,)),
            pltpu.SemaphoreType.DMA((copies,)),
            pltpu.SemaphoreType.DMA((slots + 1 + 2 * peers,)),
        ],
        compiler_params=pltpu.CompilerParams(
            collective_id=0, has_side_effects=True, vmem_limit_bytes=60 * 1024 * 1024,
        ),
        name="relay",
    )(routes, codes, w_up[0], w_down[0], cotangent)
    out, grads, up, down = pl.pallas_call(
        copy_kernel,
        out_shape=shapes,
        in_specs=[anywhere] * 4,
        out_specs=[anywhere] * 4,
        scratch_shapes=[pltpu.VMEM(a.shape, a.dtype) for a in shapes]
        + [pltpu.SemaphoreType.DMA((16,))] * 2,
        name="results",
    )(*results)
    return out, grads, up[None], down[None]


def solution(mesh):
    placed = (
        P(("section", "peer"), None),
        P(("section", "peer"), None),
        P("section", None, None),
        P("section", None, None),
        P(("section", "peer"), None),
    )
    return jax.shard_map(
        shards,
        mesh=mesh,
        in_specs=placed,
        out_specs=(
            P(("section", "peer"), None),
            P(("section", "peer"), None),
            P("section", "peer", None),
            P("section", "peer", None),
        ),
        check_vma=False,
    )
```

time: 161 us -> 129 us (0.80); the launches traced: 158 us -> 128 us
  Pallas kernels: 149 us -> 128 us
  local copies, waits for them, and re-layouts: 8.68 us -> 0 us
    pallas_call x1 -> x2, Pallas kernels: 149 us -> 128 us  [the longest x1 124 us: shards(): pl.pallas_call(kernel, out_shape=shapes, in_specs=[pl.BlockSpec(memory_sp...]
    unnamed x4 -> x0, local copies, waits for them, and re-layouts: 8.68 us -> none
where the time goes in v2:
time: 129 us; the launch traced here: 128 us
  Pallas kernels  128 us (99%)
    pallas_call x1, Pallas kernels, shards(): pl.pallas_call(kernel, out_shape=shapes, in_specs=[pl.BlockSpec(memory_sp...  124 us
    pallas_call x1, Pallas kernels, shards(): pl.pallas_call(copy_kernel, out_shape=shapes, in_specs=[anywhere] * 4, ou...  3.29 us

profile of v2, /device:TPU:1, one launch (start us, length us, event | category | flops | bytes accessed | tf_op | source)
XLA Modules:
  0.0 128.4 jit_solution(1931710964041145973)
XLA Ops:
  0.6 124.5 %relay.1 = (bf16[512,1024]{1,0:T(8,128)(2,1)}, bf16[256,1024]{1,0:T(8,128)(2,1)}, bf16[128,4096]{1,0:T(8,128)(2,1)}, bf16[512,1024]{1,0:T(8,128)(2,1)}) custom-call(s32[1,2]{1,0:T(1,128)} %routes.1, bf16[256,1024]{1,0:T(8,128)(2,1)} %codes.1, bf16[1024,4096]{1,0:T(8,128)(2,1)} %bitcast.4, bf16[4096,1024]{1,0:T(8,128)(2,1)} %bitcast.5, bf16[512,1024]{1,0:T(8,128)(2,1)} %cot.1), custom_call_target="tpu_custom_call" | custom-call | tf_op jit(solution)/shard_map/relay/pallas_call | solution.py:495
  125.1 3.3 %results.1 = (bf16[512,1024]{1,0:T(8,128)(2,1)}, bf16[256,1024]{1,0:T(8,128)(2,1)}, bf16[128,4096]{1,0:T(8,128)(2,1)}, bf16[512,1024]{1,0:T(8,128)(2,1)}) custom-call(bf16[512,1024]{1,0:T(8,128)(2,1)} %get-tuple-element.12.refs_0_, bf16[256,1024]{1,0:T(8,128)(2,1)} %get-tuple-element.13.refs_1_, bf16[128,4096]{1,0:T(8,128)(2,1)} %get-tuple-element.14.refs_2_, ...), custom_call_target="tpu_custom_call" | custom-call | tf_op jit(solution)/shard_map/results/pallas_call | solution.py:535

commit v3 on v2

v3 whole, which is shorter than its diff:
```python
import functools

import jax
import jax.numpy as jnp
from jax import lax
from jax.experimental import pallas as pl
from jax.experimental.pallas import tpu as pltpu
from jax.sharding import PartitionSpec as P

eps = 1e-05
MESH = pl.DeviceIdType.MESH
f32 = jnp.float32
bf16 = jnp.bfloat16
ROWS_ROWS = (((0,), (0,)), ((), ()))
COLS_COLS = (((1,), (1,)), ((), ()))


def dot(a, b, dims=(((1,), (0,)), ((), ()))):
    return lax.dot_general(a, b, dims, preferred_element_type=f32)


def gates(x, r):
    z = x * r
    sig = 0.5 * jnp.tanh(0.5 * z) + 0.5
    act = z * sig
    slope = sig * (1.0 + z - act)
    return act, slope


def kernel(
    routes, codes, w_up, w_down, cot,
    out, grads, up_out, down_out,
    wu, wd, codes_all, cot_own, cot_all, table_v, table_s, place, stats,
    xbuf, up_acc, down_acc, inp3, cot3, yacc, move, land,
    up_v, down_v, ig_v, home_v,
    ssem, rsem, lsem,
):
    peers = lax.axis_size("peer")
    sections = lax.axis_size("section")
    slots = cot_own.shape[0]
    nblk = codes_all.shape[1]
    blk, width = codes_all.shape[2:]
    chunks, _, cols = wu.shape
    model = chunks * cols
    ring = peers // 2
    low, high = pl.ds(0, blk // 2), pl.ds(blk // 2, blk // 2)

    sec, me = lax.axis_index("section"), lax.axis_index("peer")
    nxt, prv = lax.rem(sec + 1, sections), lax.rem(sec + sections - 1, sections)
    xi, zi = me // 2, lax.rem(me, 2)
    zo = 1 - zi

    def at(dx, z):
        return 2 * lax.rem(xi + ring + dx, ring) + z

    zp, xr, xl, op = at(0, zo), at(1, zi), at(-1, zi), at(2, zi)
    xrz, xlz, opz = at(1, zo), at(-1, zo), at(2, zo)
    order = (me, zp, xl, xr, xlz, xrz, op, opz)

    barrier = pltpu.get_barrier_semaphore()
    for d in range(1, peers):
        pl.semaphore_signal(
            barrier, inc=1, device_id=(sec, lax.rem(me + d, peers)), device_id_type=MESH
        )
    for s in (nxt, prv):
        pl.semaphore_signal(barrier, inc=1, device_id=(s, me), device_id_type=MESH)

    def local(src, dst, i):
        c = pltpu.make_async_copy(src, dst, lsem.at[i])
        c.start()
        return c

    load_first = local(cot.at[pl.ds(0, blk)], cot_all.at[0, me], slots)
    load_cot = [local(cot.at[pl.ds(k * blk, blk)], cot_own.at[k], k) for k in range(slots)]
    load_up = [
        local(w_up.at[:, pl.ds(c * cols, cols)], wu.at[c], slots + 1 + c) for c in range(chunks)
    ]
    load_down = [
        local(w_down.at[pl.ds(c * cols, cols)], wd.at[c], slots + 1 + chunks + c)
        for c in range(chunks)
    ]
    r0, r1 = routes[0, 0], routes[0, 1]
    lane = lax.broadcasted_iota(jnp.int32, (8, 128), 1)
    table_v[peers] = jnp.where(lane == 0, r0, r1)

    def remote(src, dst, i, s, p):
        return pltpu.make_async_remote_copy(
            src_ref=src, dst_ref=dst, send_sem=ssem.at[i], recv_sem=rsem.at[i],
            device_id=(s, p), device_id_type=MESH,
        )

    sent = []

    def send(src, dst, i, s, p):
        c = remote(src, dst, i, s, p)
        c.start()
        sent.append(c)

    def arrived(dst, i):
        remote(dst, dst, i, sec, zp).wait_recv()

    FIRST, MORE = nblk, nblk + 1
    pieces = nblk + 2
    HOP = 7 * pieces
    ROUTE_HOP = HOP + nblk
    ROUTE = ROUTE_HOP + 1
    STAT = ROUTE + peers
    UPS = STAT + peers
    HOME = UPS + peers
    PACK = HOME + 1

    pl.semaphore_wait(barrier, peers + 1)

    def chunk(g, owner):
        if g < nblk:
            return codes_all.at[owner, g]
        return cot_all.at[g - nblk, owner]

    def pass_on(g, owner, o, p):
        send(chunk(g, owner), chunk(g, owner), 7 * g + o - 1, sec, p)

    def start_across(g):
        pass_on(g, me, 1, zp)

    def start_along(g):
        pass_on(g, me, 2, xr)
        pass_on(g, me, 3, xl)

    def wait_for(g, *numbers):
        for o in numbers:
            arrived(chunk(g, order[o]), 7 * g + o - 1)

    def pass_partner(g):
        wait_for(g, 1)
        pass_on(g, zp, 4, xr)
        pass_on(g, zp, 5, xl)

    def pass_opposite(g):
        if g % 2 == 0:
            wait_for(g, 2)
            pass_on(g, xl, 6, xr)
        else:
            wait_for(g, 3)
            pass_on(g, xr, 6, xl)

    def pass_across(g):
        wait_for(g, 6)
        pass_on(g, op, 7, zp)

    send(table_v.at[peers], table_v.at[me], ROUTE_HOP, nxt, me)
    for b in range(nblk):
        send(codes.at[pl.ds(b * blk, blk)], codes_all.at[me, b], HOP + b, nxt, me)
    load_first.wait()
    start_along(FIRST)
    arrived(table_v.at[me], ROUTE_HOP)
    for d in range(1, peers):
        send(table_v.at[me], table_v.at[me], ROUTE + d, sec, lax.rem(me + d, peers))

    for d in range(1, peers):
        j = lax.rem(me + d, peers)
        arrived(table_v.at[j], ROUTE + peers - d)
    fetch = local(table_v, table_s, slots)
    fetch.wait()

    counts = [0] * peers
    slot_block, slot_live = [0] * slots, [0] * slots
    targets = []
    for p in range(peers):
        for b in range(nblk):
            q = table_s[p, 0, b]
            k = 0
            for n in range(peers):
                k = jnp.where(q == n, counts[n], k)
                counts[n] = counts[n] + jnp.where(q == n, 1, 0)
            for n in range(slots):
                here = (q == me) & (k == n)
                slot_block[n] = jnp.where(here, nblk * p + b, slot_block[n])
                slot_live[n] = jnp.where(here, 1, slot_live[n])
            targets.append((q, k))
    before = [0]
    for n in range(peers - 1):
        before.append(before[n] + counts[n] - 1)
    own_before = 0
    for n in range(peers):
        own_before = jnp.where(me == n, before[n], own_before)
    for n, (q, k) in enumerate(targets):
        ahead = 0
        for m in range(peers):
            ahead = jnp.where(q == m, before[m], ahead)
        place[n] = jnp.clip(jnp.where(k == 0, q, peers + ahead + k - 1), 0, 2 * peers - 1)

    for c in load_cot:
        c.wait()

    def mine(j):
        rows = jnp.zeros((blk, width), bf16)
        for k in range(1, slots):
            hit = (slot_live[k] == 1) & (own_before + k - 1 == j)
            rows = jnp.where(hit, cot_own[k], rows)
        return rows

    move[0] = mine(opz)
    send(move.at[0], land.at[0], PACK + 0, sec, zp)
    move[5] = mine(xrz)
    send(move.at[5], land.at[5], PACK + 5, sec, xr)
    move[6] = mine(xlz)
    send(move.at[6], land.at[6], PACK + 6, sec, xl)
    arrived(codes_all.at[me, 0], HOP)
    start_along(0)
    start_across(0)
    arrived(land.at[0], PACK + 0)
    move[1] = mine(op) + land[0]
    send(move.at[1, low], land.at[1, low], PACK + 1, sec, xr)
    send(move.at[1, high], land.at[1, high], PACK + 2, sec, xl)
    for b in range(1, nblk):
        arrived(codes_all.at[me, b], HOP + b)
        start_along(b)

    two = nblk * blk
    xs, ds = pl.ds(0, two), pl.ds(two, two)

    for c in load_up:
        c.wait()

    def x2_step(c, ssq):
        rows = jnp.concatenate([codes_all[me, b] for b in range(nblk)], axis=0)
        x = dot(rows, wu[c])
        xbuf[c, xs] = x
        return ssq + jnp.sum(x * x, axis=-1, keepdims=True)

    ssq = lax.fori_loop(0, chunks, x2_step, jnp.zeros((two, 1), f32))
    r2 = lax.rsqrt(ssq * (1.0 / model) + eps)

    arrived(land.at[1, low], PACK + 1)
    arrived(land.at[1, high], PACK + 2)
    move[3] = mine(xr)
    move[3, low] = move[3, low] + land[1, low]
    send(move.at[3], land.at[3], PACK + 3, sec, xr)
    move[4] = mine(xl)
    move[4, high] = move[4, high] + land[1, high]
    send(move.at[4], land.at[4], PACK + 4, sec, xl)
    arrived(land.at[5], PACK + 5)
    arrived(land.at[6], PACK + 6)
    move[2] = mine(zp) + land[5] + land[6]
    send(move.at[2], land.at[2], PACK + 7, sec, zp)
    start_across(FIRST)
    pass_opposite(FIRST)
    for b in range(1, nblk):
        start_across(b)

    def slope_step(c, carry):
        xbuf[c, ds] = gates(xbuf[c, xs], r2)[1]
        return carry

    lax.fori_loop(0, chunks, slope_step, 0)

    arrived(land.at[3], PACK + 3)
    arrived(land.at[4], PACK + 4)
    arrived(land.at[2], PACK + 7)
    cot_all[1, me] = mine(me) + land[3] + land[4] + land[2]
    start_along(MORE)
    start_across(MORE)
    pass_partner(FIRST)
    pass_across(FIRST)
    pass_opposite(MORE)
    pass_partner(MORE)
    for g in range(nblk):
        pass_opposite(g)
    pass_partner(0)
    pass_across(MORE)
    for g in range(1, nblk):
        pass_partner(g)

    eye = lax.broadcasted_iota(jnp.int32, (blk, blk), 0) == lax.broadcasted_iota(
        jnp.int32, (blk, blk), 1
    )

    def as_row(col):
        return jnp.sum(jnp.where(eye, col, 0.0), axis=0, keepdims=True)

    def as_col(row):
        return jnp.sum(jnp.where(eye, row, 0.0), axis=1, keepdims=True)

    def cot_block(n):
        i = place[n]
        return cot_all[i // peers, lax.rem(i, peers)]

    for c in load_down:
        c.wait()
    wait_for(FIRST, 3, 4, 5, 7)
    wait_for(MORE, 2, 4, 5, 7)
    for b in range(nblk):
        cot3[pl.ds(b * blk, blk)] = cot_block(nblk * me + b)

    def dz_step(c, m):
        dz = xbuf[c, ds] * dot(cot3[xs], wd[c], COLS_COLS)
        xbuf[c, ds] = dz
        return m + jnp.sum(xbuf[c, xs] * dz, axis=-1, keepdims=True)

    m2 = lax.fori_loop(0, chunks, dz_step, jnp.zeros((two, 1), f32)) * (1.0 / model)
    c2 = (r2 * r2 * r2) * m2
    rows = [as_row(v[b * blk : (b + 1) * blk]) for v in (r2, c2) for b in range(nblk)]
    stats[me] = jnp.concatenate(rows + [jnp.zeros((8 - 2 * nblk, blk), f32)], axis=0)
    for d in range(1, peers):
        send(stats.at[me], stats.at[me], STAT + d, sec, lax.rem(me + d, peers))
    for g in range(nblk):
        pass_across(g)

    yacc[xs] = cot3[xs].astype(f32)

    def home_step(c, carry):
        dx = (r2 * xbuf[c, ds] - xbuf[c, xs] * c2).astype(bf16)
        yacc[xs] += dot(dx, wu[c], COLS_COLS)
        return carry

    lax.fori_loop(0, chunks, home_step, 0)
    ig_v[...] = yacc[xs].astype(bf16)
    send(ig_v, home_v, HOME, prv, me)
    for d in range(1, peers):
        j = lax.rem(me + d, peers)
        arrived(stats.at[j], STAT + peers - d)

    up_acc[...] = jnp.zeros_like(up_acc)
    down_acc[...] = jnp.zeros_like(down_acc)

    def owner_of(o):
        q = order[0]
        for n in range(1, peers):
            q = jnp.where(o == n, order[n], q)
        return q

    def pair_step(i, carry):
        rs, cs = [], []
        for n in range(2):
            p = owner_of(2 * i + n)
            for b in range(nblk):
                part = pl.ds((nblk * n + b) * blk, blk)
                inp3[part] = codes_all[p, b]
                cot3[part] = cot_block(nblk * p + b)
            tile = stats[p]
            rs += [as_col(tile[b : b + 1]) for b in range(nblk)]
            cs += [as_col(tile[nblk + b : nblk + b + 1]) for b in range(nblk)]
        r, c3 = jnp.concatenate(rs, axis=0), jnp.concatenate(cs, axis=0)
        x = dot(inp3[...], wu[me])
        act, slope = gates(x, r)
        act = act.astype(bf16)
        back = dot(cot3[...], wd[me], COLS_COLS)
        dx = (r * (back * slope) - x * c3).astype(bf16)
        up_acc[...] += dot(inp3[...], dx, ROWS_ROWS)
        down_acc[...] += dot(act, cot3[...], ROWS_ROWS)
        return carry

    for g in range(nblk):
        wait_for(g, 3 if g % 2 == 0 else 2)
    lax.fori_loop(0, 2, pair_step, 0)
    for g in range(nblk):
        wait_for(g, 4, 5)
    lax.fori_loop(2, 3, pair_step, 0)
    for g in range(nblk):
        wait_for(g, 7)
    lax.fori_loop(3, peers // 2, pair_step, 0)

    saves = []
    factor = 1.0 / (peers * nblk)
    tall = width // peers
    up_v[...] = (up_acc[...] * factor).astype(bf16)
    for d in range(1, peers):
        j = lax.rem(me + d, peers)
        send(
            up_v.at[pl.ds(pl.multiple_of(j * tall, tall), tall)],
            up_out.at[:, pl.ds(pl.multiple_of(me * cols, cols), cols)],
            UPS + d, sec, j,
        )
    saves.append(local(
        up_v.at[pl.ds(pl.multiple_of(me * tall, tall), tall)],
        up_out.at[:, pl.ds(pl.multiple_of(me * cols, cols), cols)], 0,
    ))
    down_v[...] = (down_acc[...] * factor).astype(bf16)
    saves.append(local(down_v, down_out, 1))

    for k in range(slots):
        rows = codes_all[slot_block[k] // nblk, lax.rem(slot_block[k], nblk)]
        inp3[pl.ds(k * blk, blk)] = jnp.where(slot_live[k] == 1, rows, jnp.zeros_like(rows))

    def x_step(c, ssq):
        x = dot(inp3[...], wu[c])
        xbuf[c] = x
        return ssq + jnp.sum(x * x, axis=-1, keepdims=True)

    ssq = lax.fori_loop(0, chunks, x_step, jnp.zeros((slots * blk, 1), f32))
    r = lax.rsqrt(ssq * (1.0 / model) + eps)
    arrived(home_v, HOME)
    saves.append(local(home_v, grads, 2))
    yacc[...] = inp3[...].astype(f32)

    def y_step(c, carry):
        act, _ = gates(xbuf[c], r)
        yacc[...] += dot(act.astype(bf16), wd[c])
        return carry

    lax.fori_loop(0, chunks, y_step, 0)
    cot3[...] = yacc[...].astype(bf16)
    saves.append(local(cot3, out, 3))

    for d in range(1, peers):
        j = lax.rem(me + peers - d, peers)
        arrived(up_out.at[:, pl.ds(pl.multiple_of(j * cols, cols), cols)], UPS + d)
    for c in saves:
        c.wait()
    for c in sent:
        c.wait_send()


def copy_kernel(*refs):
    n = (len(refs) - 2) // 3
    sources, results, held = refs[:n], refs[n : 2 * n], refs[2 * n : 3 * n]
    in_sem, out_sem = refs[3 * n :]
    loads = []
    for src, mid in zip(sources, held):
        rows = src.shape[0] // 4
        for k in range(4):
            part = pl.ds(k * rows, rows)
            loads.append(pltpu.make_async_copy(src.at[part], mid.at[part], in_sem.at[len(loads)]))
    for c in loads:
        c.start()
    stores = []
    for mid, dst in zip(held, results):
        rows = dst.shape[0] // 4
        for k in range(4):
            part = pl.ds(k * rows, rows)
            loads[len(stores)].wait()
            c = pltpu.make_async_copy(mid.at[part], dst.at[part], out_sem.at[len(stores)])
            c.start()
            stores.append(c)
    for c in stores:
        c.wait()


def shards(codes, routes, w_up, w_down, cotangent):
    peers = lax.axis_size("peer")
    nblk = routes.shape[1]
    rows, width = codes.shape
    blk = rows // nblk
    slots = cotangent.shape[0] // blk
    model = w_up.shape[2]
    cols = model // peers
    anywhere = pl.BlockSpec(memory_space=pl.ANY)
    copies = 7 * (nblk + 2) + nblk + 2 + 3 * peers + 8
    shapes = (
        jax.ShapeDtypeStruct((slots * blk, width), bf16),
        jax.ShapeDtypeStruct((rows, width), bf16),
        jax.ShapeDtypeStruct((width // peers, model), bf16),
        jax.ShapeDtypeStruct((cols, width), bf16),
    )
    results = pl.pallas_call(
        kernel,
        out_shape=shapes,
        in_specs=[pl.BlockSpec(memory_space=pltpu.SMEM)] + [anywhere] * 4,
        out_specs=[anywhere] * 4,
        scratch_shapes=[
            pltpu.VMEM((peers, width, cols), bf16),
            pltpu.VMEM((peers, cols, width), bf16),
            pltpu.VMEM((peers, nblk, blk, width), bf16),
            pltpu.VMEM((slots, blk, width), bf16),
            pltpu.VMEM((2, peers, blk, width), bf16),
            pltpu.VMEM((peers + 1, 8, 128), jnp.int32),
            pltpu.SMEM((peers + 1, 8, 128), jnp.int32),
            pltpu.SMEM((2 * peers,), jnp.int32),
            pltpu.VMEM((peers, 8, blk), f32),
            pltpu.VMEM((peers, slots * blk, cols), f32),
            pltpu.VMEM((width, cols), f32),
            pltpu.VMEM((cols, width), f32),
            pltpu.VMEM((slots * blk, width), bf16),
            pltpu.VMEM((slots * blk, width), bf16),
            pltpu.VMEM((slots * blk, width), f32),
            pltpu.VMEM((7, blk, width), bf16),
            pltpu.VMEM((7, blk, width), bf16),
            pltpu.VMEM((width, cols), bf16),
            pltpu.VMEM((cols, width), bf16),
            pltpu.VMEM((rows, width), bf16),
            pltpu.VMEM((rows, width), bf16),
            pltpu.SemaphoreType.DMA((copies,)),
            pltpu.SemaphoreType.DMA((copies,)),
            pltpu.SemaphoreType.DMA((slots + 1 + 2 * peers,)),
        ],
        compiler_params=pltpu.CompilerParams(
            collective_id=0, has_side_effects=True, vmem_limit_bytes=62 * 1024 * 1024,
        ),
        name="relay",
    )(routes, codes, w_up[0], w_down[0], cotangent)
    out, grads, up, down = pl.pallas_call(
        copy_kernel,
        out_shape=shapes,
        in_specs=[anywhere] * 4,
        out_specs=[anywhere] * 4,
        scratch_shapes=[pltpu.VMEM(a.shape, a.dtype) for a in shapes]
        + [pltpu.SemaphoreType.DMA((16,))] * 2,
        name="results",
    )(*results)
    return out, grads, up[None], down[None]


def solution(mesh):
    placed = (
        P(("section", "peer"), None),
        P(("section", "peer"), None),
        P("section", None, None),
        P("section", None, None),
        P(("section", "peer"), None),
    )
    return jax.shard_map(
        shards,
        mesh=mesh,
        in_specs=placed,
        out_specs=(
            P(("section", "peer"), None),
            P(("section", "peer"), None),
            P("section", "peer", None),
            P("section", "peer", None),
        ),
        check_vma=False,
    )
```

time: 129 us -> 117 us (0.907)
  the two profiles are of different devices: /device:TPU:1 before, /device:TPU:18 now
where the time goes in v3:
time: 117 us
  Pallas kernels  116 us (99%)
    pallas_call x1, Pallas kernels, shards(): pl.pallas_call(kernel, out_shape=shapes, in_specs=[pl.BlockSpec(memory_sp...  113 us
    pallas_call x1, Pallas kernels, shards(): pl.pallas_call(copy_kernel, out_shape=shapes, in_specs=[anywhere] * 4, ou...  3.29 us

profile of v3, /device:TPU:18, one launch (start us, length us, event | category | flops | bytes accessed | tf_op | source)
XLA Modules:
  0.0 116.8 jit_solution(7307437320052041235)
XLA Ops:
  0.6 112.8 %relay.1 = (bf16[512,1024]{1,0:T(8,128)(2,1)}, bf16[256,1024]{1,0:T(8,128)(2,1)}, bf16[128,4096]{1,0:T(8,128)(2,1)}, bf16[512,1024]{1,0:T(8,128)(2,1)}) custom-call(s32[1,2]{1,0:T(1,128)} %routes.1, bf16[256,1024]{1,0:T(8,128)(2,1)} %codes.1, bf16[1024,4096]{1,0:T(8,128)(2,1)} %bitcast.4, bf16[4096,1024]{1,0:T(8,128)(2,1)} %bitcast.5, bf16[512,1024]{1,0:T(8,128)(2,1)} %cot.1), custom_call_target="tpu_custom_call" | custom-call | tf_op jit(solution)/shard_map/relay/pallas_call | solution.py:455
  113.5 3.3 %results.1 = (bf16[512,1024]{1,0:T(8,128)(2,1)}, bf16[256,1024]{1,0:T(8,128)(2,1)}, bf16[128,4096]{1,0:T(8,128)(2,1)}, bf16[512,1024]{1,0:T(8,128)(2,1)}) custom-call(bf16[512,1024]{1,0:T(8,128)(2,1)} %get-tuple-element.12.refs_0_, bf16[256,1024]{1,0:T(8,128)(2,1)} %get-tuple-element.13.refs_1_, bf16[128,4096]{1,0:T(8,128)(2,1)} %get-tuple-element.14.refs_2_, ...), custom_call_target="tpu_custom_call" | custom-call | tf_op jit(solution)/shard_map/results/pallas_call | solution.py:491

commit v4 on v3

--- a/solution.py
+++ b/solution.py
@@ -55,6 +55,13 @@
 
     zp, xr, xl, op = at(0, zo), at(1, zi), at(-1, zi), at(2, zi)
     xrz, xlz, opz = at(1, zo), at(-1, zo), at(2, zo)
+    cross_out = lax.rem(sec, 2)
+    cross_in = 1 - cross_out
+
+    def crossed(p, cross):
+        return p + cross * (1 - 2 * (p % 2 if isinstance(p, int) else lax.rem(p, 2)))
+
+    there, sender = crossed(me, cross_out), crossed(me, cross_in)
     order = (me, zp, xl, xr, xlz, xrz, op, opz)
 
     barrier = pltpu.get_barrier_semaphore()
@@ -63,13 +70,15 @@
             barrier, inc=1, device_id=(sec, lax.rem(me + d, peers)), device_id_type=MESH
         )
     for s in (nxt, prv):
-        pl.semaphore_signal(barrier, inc=1, device_id=(s, me), device_id_type=MESH)
+        for p in range(peers):
+            pl.semaphore_signal(barrier, inc=1, device_id=(s, p), device_id_type=MESH)
 
     def local(src, dst, i):
         c = pltpu.make_async_copy(src, dst, lsem.at[i])
         c.start()
         return c
 
+    load_codes = local(codes, ig_v, slots + 1 + 2 * chunks)
     load_first = local(cot.at[pl.ds(0, blk)], cot_all.at[0, me], slots)
     load_cot = [local(cot.at[pl.ds(k * blk, blk)], cot_own.at[k], k) for k in range(slots)]
     load_up = [
@@ -102,14 +111,13 @@
     FIRST, MORE = nblk, nblk + 1
     pieces = nblk + 2
     HOP = 7 * pieces
-    ROUTE_HOP = HOP + nblk
-    ROUTE = ROUTE_HOP + 1
+    ROUTE = HOP + nblk
     STAT = ROUTE + peers
     UPS = STAT + peers
     HOME = UPS + peers
     PACK = HOME + 1
 
-    pl.semaphore_wait(barrier, peers + 1)
+    pl.semaphore_wait(barrier, 3 * peers - 1)
 
     def chunk(g, owner):
         if g < nblk:
@@ -147,18 +155,19 @@
         wait_for(g, 6)
         pass_on(g, op, 7, zp)
 
-    send(table_v.at[peers], table_v.at[me], ROUTE_HOP, nxt, me)
+    for d in range(peers):
+        send(table_v.at[peers], table_v.at[me], ROUTE + d, nxt, lax.rem(me + d, peers))
+    load_codes.wait()
     for b in range(nblk):
-        send(codes.at[pl.ds(b * blk, blk)], codes_all.at[me, b], HOP + b, nxt, me)
+        send(ig_v.at[pl.ds(b * blk, blk)], codes_all.at[there, b], HOP + b, nxt, there)
+    codes_sent = sent[-nblk:]
+    del sent[-nblk:]
     load_first.wait()
     start_along(FIRST)
-    arrived(table_v.at[me], ROUTE_HOP)
-    for d in range(1, peers):
-        send(table_v.at[me], table_v.at[me], ROUTE + d, sec, lax.rem(me + d, peers))
-
-    for d in range(1, peers):
+
+    for d in range(peers):
         j = lax.rem(me + d, peers)
-        arrived(table_v.at[j], ROUTE + peers - d)
+        arrived(table_v.at[j], ROUTE + (peers - d) % peers)
     fetch = local(table_v, table_s, slots)
     fetch.wait()
 
@@ -174,7 +183,7 @@
                 counts[n] = counts[n] + jnp.where(q == n, 1, 0)
             for n in range(slots):
                 here = (q == me) & (k == n)
-                slot_block[n] = jnp.where(here, nblk * p + b, slot_block[n])
+                slot_block[n] = jnp.where(here, nblk * crossed(p, cross_in) + b, slot_block[n])
                 slot_live[n] = jnp.where(here, 1, slot_live[n])
             targets.append((q, k))
     before = [0]
@@ -199,28 +208,47 @@
             rows = jnp.where(hit, cot_own[k], rows)
         return rows
 
-    move[0] = mine(opz)
-    send(move.at[0], land.at[0], PACK + 0, sec, zp)
-    move[5] = mine(xrz)
-    send(move.at[5], land.at[5], PACK + 5, sec, xr)
-    move[6] = mine(xlz)
-    send(move.at[6], land.at[6], PACK + 6, sec, xl)
-    arrived(codes_all.at[me, 0], HOP)
-    start_along(0)
-    start_across(0)
-    arrived(land.at[0], PACK + 0)
-    move[1] = mine(op) + land[0]
-    send(move.at[1, low], land.at[1, low], PACK + 1, sec, xr)
-    send(move.at[1, high], land.at[1, high], PACK + 2, sec, xl)
-    for b in range(1, nblk):
-        arrived(codes_all.at[me, b], HOP + b)
-        start_along(b)
+    def pack_start():
+        move[0] = mine(opz)
+        send(move.at[0], land.at[0], PACK + 0, sec, zp)
+        move[5] = mine(xrz)
+        send(move.at[5], land.at[5], PACK + 5, sec, xr)
+        move[6] = mine(xlz)
+        send(move.at[6], land.at[6], PACK + 6, sec, xl)
+
+    def pack_far():
+        arrived(land.at[0], PACK + 0)
+        move[1] = mine(op) + land[0]
+        send(move.at[1, low], land.at[1, low], PACK + 1, sec, xr)
+        send(move.at[1, high], land.at[1, high], PACK + 2, sec, xl)
+
+    def pack_along():
+        arrived(land.at[1, low], PACK + 1)
+        arrived(land.at[1, high], PACK + 2)
+        move[3] = mine(xr)
+        move[3, low] = move[3, low] + land[1, low]
+        send(move.at[3], land.at[3], PACK + 3, sec, xr)
+        move[4] = mine(xl)
+        move[4, high] = move[4, high] + land[1, high]
+        send(move.at[4], land.at[4], PACK + 4, sec, xl)
+
+    def pack_across():
+        arrived(land.at[5], PACK + 5)
+        arrived(land.at[6], PACK + 6)
+        move[2] = mine(zp) + land[5] + land[6]
+        send(move.at[2], land.at[2], PACK + 7, sec, zp)
+
+    def pack_end():
+        arrived(land.at[3], PACK + 3)
+        arrived(land.at[4], PACK + 4)
+        arrived(land.at[2], PACK + 7)
+        cot_all[1, me] = mine(me) + land[3] + land[4] + land[2]
+
+    def codes_here(g):
+        arrived(codes_all.at[me, g], HOP + g)
 
     two = nblk * blk
     xs, ds = pl.ds(0, two), pl.ds(two, two)
-
-    for c in load_up:
-        c.wait()
 
     def x2_step(c, ssq):
         rows = jnp.concatenate([codes_all[me, b] for b in range(nblk)], axis=0)
@@ -228,48 +256,38 @@
         xbuf[c, xs] = x
         return ssq + jnp.sum(x * x, axis=-1, keepdims=True)
 
+    def slope_step(c, r):
+        xbuf[c, ds] = gates(xbuf[c, xs], r)[1]
+        return r
+
+    pack_start()
+    codes_here(0)
+    start_along(0)
+    start_across(0)
+    pack_far()
+    codes_here(1)
+    start_along(1)
+    for c in load_up:
+        c.wait()
     ssq = lax.fori_loop(0, chunks, x2_step, jnp.zeros((two, 1), f32))
     r2 = lax.rsqrt(ssq * (1.0 / model) + eps)
-
-    arrived(land.at[1, low], PACK + 1)
-    arrived(land.at[1, high], PACK + 2)
-    move[3] = mine(xr)
-    move[3, low] = move[3, low] + land[1, low]
-    send(move.at[3], land.at[3], PACK + 3, sec, xr)
-    move[4] = mine(xl)
-    move[4, high] = move[4, high] + land[1, high]
-    send(move.at[4], land.at[4], PACK + 4, sec, xl)
-    arrived(land.at[5], PACK + 5)
-    arrived(land.at[6], PACK + 6)
-    move[2] = mine(zp) + land[5] + land[6]
-    send(move.at[2], land.at[2], PACK + 7, sec, zp)
+    pack_along()
+    pack_across()
     start_across(FIRST)
     pass_opposite(FIRST)
-    for b in range(1, nblk):
-        start_across(b)
-
-    def slope_step(c, carry):
-        xbuf[c, ds] = gates(xbuf[c, xs], r2)[1]
-        return carry
-
-    lax.fori_loop(0, chunks, slope_step, 0)
-
-    arrived(land.at[3], PACK + 3)
-    arrived(land.at[4], PACK + 4)
-    arrived(land.at[2], PACK + 7)
-    cot_all[1, me] = mine(me) + land[3] + land[4] + land[2]
+    start_across(1)
+    lax.fori_loop(0, chunks, slope_step, r2)
+    pack_end()
     start_along(MORE)
     start_across(MORE)
     pass_partner(FIRST)
     pass_across(FIRST)
     pass_opposite(MORE)
     pass_partner(MORE)
-    for g in range(nblk):
-        pass_opposite(g)
+    pass_opposite(0)
+    pass_opposite(1)
     pass_partner(0)
     pass_across(MORE)
-    for g in range(1, nblk):
-        pass_partner(g)
 
     eye = lax.broadcasted_iota(jnp.int32, (blk, blk), 0) == lax.broadcasted_iota(
         jnp.int32, (blk, blk), 1
@@ -290,7 +308,7 @@
     wait_for(FIRST, 3, 4, 5, 7)
     wait_for(MORE, 2, 4, 5, 7)
     for b in range(nblk):
-        cot3[pl.ds(b * blk, blk)] = cot_block(nblk * me + b)
+        cot3[pl.ds(b * blk, blk)] = cot_block(nblk * sender + b)
 
     def dz_step(c, m):
         dz = xbuf[c, ds] * dot(cot3[xs], wd[c], COLS_COLS)
@@ -303,6 +321,7 @@
     stats[me] = jnp.concatenate(rows + [jnp.zeros((8 - 2 * nblk, blk), f32)], axis=0)
     for d in range(1, peers):
         send(stats.at[me], stats.at[me], STAT + d, sec, lax.rem(me + d, peers))
+    pass_partner(1)
     for g in range(nblk):
         pass_across(g)
 
@@ -314,8 +333,10 @@
         return carry
 
     lax.fori_loop(0, chunks, home_step, 0)
+    for c in codes_sent:
+        c.wait_send()
     ig_v[...] = yacc[xs].astype(bf16)
-    send(ig_v, home_v, HOME, prv, me)
+    send(ig_v, home_v, HOME, prv, sender)
     for d in range(1, peers):
         j = lax.rem(me + d, peers)
         arrived(stats.at[j], STAT + peers - d)
@@ -336,7 +357,7 @@
             for b in range(nblk):
                 part = pl.ds((nblk * n + b) * blk, blk)
                 inp3[part] = codes_all[p, b]
-                cot3[part] = cot_block(nblk * p + b)
+                cot3[part] = cot_block(nblk * crossed(p, cross_in) + b)
             tile = stats[p]
             rs += [as_col(tile[b : b + 1]) for b in range(nblk)]
             cs += [as_col(tile[nblk + b : nblk + b + 1]) for b in range(nblk)]
@@ -364,8 +385,8 @@
     factor = 1.0 / (peers * nblk)
     tall = width // peers
     up_v[...] = (up_acc[...] * factor).astype(bf16)
-    for d in range(1, peers):
-        j = lax.rem(me + d, peers)
+    for j in reversed(order[1:]):
+        d = lax.rem(j + peers - me, peers)
         send(
             up_v.at[pl.ds(pl.multiple_of(j * tall, tall), tall)],
             up_out.at[:, pl.ds(pl.multiple_of(me * cols, cols), cols)],
@@ -481,7 +502,7 @@
             pltpu.VMEM((rows, width), bf16),
             pltpu.SemaphoreType.DMA((copies,)),
             pltpu.SemaphoreType.DMA((copies,)),
-            pltpu.SemaphoreType.DMA((slots + 1 + 2 * peers,)),
+            pltpu.SemaphoreType.DMA((slots + 2 + 2 * peers,)),
         ],
         compiler_params=pltpu.CompilerParams(
             collective_id=0, has_side_effects=True, vmem_limit_bytes=62 * 1024 * 1024,

time: 117 us -> 110 us (0.940)
  the two profiles are of different devices: /device:TPU:18 before, /device:TPU:1 now
where the time goes in v4:
time: 110 us
  Pallas kernels  110 us (100%)
    pallas_call x1, Pallas kernels, shards(): pl.pallas_call(kernel, out_shape=shapes, in_specs=[pl.BlockSpec(memory_sp...  106 us
    pallas_call x1, Pallas kernels, shards(): pl.pallas_call(copy_kernel, out_shape=shapes, in_specs=[anywhere] * 4, ou...  3.29 us

profile of v4, /device:TPU:1, one launch (start us, length us, event | category | flops | bytes accessed | tf_op | source)
XLA Modules:
  0.0 110.3 jit_solution(3397670695845139379)
XLA Ops:
  0.6 106.3 %relay.1 = (bf16[512,1024]{1,0:T(8,128)(2,1)}, bf16[256,1024]{1,0:T(8,128)(2,1)}, bf16[128,4096]{1,0:T(8,128)(2,1)}, bf16[512,1024]{1,0:T(8,128)(2,1)}) custom-call(s32[1,2]{1,0:T(1,128)} %routes.1, bf16[256,1024]{1,0:T(8,128)(2,1)} %codes.1, bf16[1024,4096]{1,0:T(8,128)(2,1)} %bitcast.4, bf16[4096,1024]{1,0:T(8,128)(2,1)} %bitcast.5, bf16[512,1024]{1,0:T(8,128)(2,1)} %cot.1), custom_call_target="tpu_custom_call" | custom-call | tf_op jit(solution)/shard_map/relay/pallas_call | solution.py:476
  107.0 3.3 %results.1 = (bf16[512,1024]{1,0:T(8,128)(2,1)}, bf16[256,1024]{1,0:T(8,128)(2,1)}, bf16[128,4096]{1,0:T(8,128)(2,1)}, bf16[512,1024]{1,0:T(8,128)(2,1)}) custom-call(bf16[512,1024]{1,0:T(8,128)(2,1)} %get-tuple-element.12.refs_0_, bf16[256,1024]{1,0:T(8,128)(2,1)} %get-tuple-element.13.refs_1_, bf16[128,4096]{1,0:T(8,128)(2,1)} %get-tuple-element.14.refs_2_, ...), custom_call_target="tpu_custom_call" | custom-call | tf_op jit(solution)/shard_map/results/pallas_call | solution.py:512

commit v5 on v4

--- a/solution.py
+++ b/solution.py
@@ -315,7 +315,7 @@
         xbuf[c, ds] = dz
         return m + jnp.sum(xbuf[c, xs] * dz, axis=-1, keepdims=True)
 
-    m2 = lax.fori_loop(0, chunks, dz_step, jnp.zeros((two, 1), f32)) * (1.0 / model)
+    m2 = lax.fori_loop(0, chunks, dz_step, jnp.zeros((two, 1), f32), unroll=2) * (1.0 / model)
     c2 = (r2 * r2 * r2) * m2
     rows = [as_row(v[b * blk : (b + 1) * blk]) for v in (r2, c2) for b in range(nblk)]
     stats[me] = jnp.concatenate(rows + [jnp.zeros((8 - 2 * nblk, blk), f32)], axis=0)
@@ -332,7 +332,7 @@
         yacc[xs] += dot(dx, wu[c], COLS_COLS)
         return carry
 
-    lax.fori_loop(0, chunks, home_step, 0)
+    lax.fori_loop(0, chunks, home_step, 0, unroll=2)
     for c in codes_sent:
         c.wait_send()
     ig_v[...] = yacc[xs].astype(bf16)

time: 110 us -> 110 us (level)
  no operation moved by 1% of the time
where the time goes in v5:
time: 110 us
  Pallas kernels  110 us (100%)
    pallas_call x1, Pallas kernels, shards(): pl.pallas_call(kernel, out_shape=shapes, in_specs=[pl.BlockSpec(memory_sp...  106 us
    pallas_call x1, Pallas kernels, shards(): pl.pallas_call(copy_kernel, out_shape=shapes, in_specs=[anywhere] * 4, ou...  3.29 us

profile of v5, /device:TPU:1, one launch (start us, length us, event | category | flops | bytes accessed | tf_op | source)
XLA Modules:
  0.0 110.2 jit_solution(15926786647104366430)
XLA Ops:
  0.6 106.3 %relay.1 = (bf16[512,1024]{1,0:T(8,128)(2,1)}, bf16[256,1024]{1,0:T(8,128)(2,1)}, bf16[128,4096]{1,0:T(8,128)(2,1)}, bf16[512,1024]{1,0:T(8,128)(2,1)}) custom-call(s32[1,2]{1,0:T(1,128)} %routes.1, bf16[256,1024]{1,0:T(8,128)(2,1)} %codes.1, bf16[1024,4096]{1,0:T(8,128)(2,1)} %bitcast.4, bf16[4096,1024]{1,0:T(8,128)(2,1)} %bitcast.5, bf16[512,1024]{1,0:T(8,128)(2,1)} %cot.1), custom_call_target="tpu_custom_call" | custom-call | tf_op jit(solution)/shard_map/relay/pallas_call | solution.py:476
  107.0 3.3 %results.1 = (bf16[512,1024]{1,0:T(8,128)(2,1)}, bf16[256,1024]{1,0:T(8,128)(2,1)}, bf16[128,4096]{1,0:T(8,128)(2,1)}, bf16[512,1024]{1,0:T(8,128)(2,1)}) custom-call(bf16[512,1024]{1,0:T(8,128)(2,1)} %get-tuple-element.12.refs_0_, bf16[256,1024]{1,0:T(8,128)(2,1)} %get-tuple-element.13.refs_1_, bf16[128,4096]{1,0:T(8,128)(2,1)} %get-tuple-element.14.refs_2_, ...), custom_call_target="tpu_custom_call" | custom-call | tf_op jit(solution)/shard_map/results/pallas_call | solution.py:512
